TPU v7x, 256 devices: a whole 4x4x8 slice. The times are simulated.
256 devices in a mesh: pool: 2 (over x_lo), ep: 128 (over y, x_hi, z, core).
Axes of the slice: x: 4 (x_hi: 2, x_lo: 2; x = x_hi * 2 + x_lo), y: 4, z: 8, core: 2. Of those that a mesh axis runs over, the one named last changes fastest.
Arguments:
- cache: bfloat16 [2, 256, 128, 576], P('pool', None, 'ep'), may hold values from -448 to 448, as said below
- cache_scale: bfloat16 [2, 256, 128, 4], P('pool', None, 'ep'), may hold values from 0.0006980896 to 0.0069885254
- lengths: int32 [2, 256], replicated, may hold values from 1 to 128, 10922 in all within a row
- assign: int32 [2, 256], replicated, may hold values from 0 to 255, each once within a row
- queries: bfloat16 [2, 256, 4, 64, 576], P('pool', 'ep'), may hold values from -360 to 360
- new_kv: bfloat16 [2, 256, 4, 576], P('pool', 'ep'), may hold values from -6 to 6
- hidden: bfloat16 [2, 256, 4, 3584], P('pool', 'ep'), may hold values from -6 to 6
- expert_ids: int32 [2, 256, 4, 8], P('pool', 'ep'), may hold values from 0 to 127, all different within a row; in each aligned block of 8 rows (0 to 7, 8 to 15, ..., all dimensions but the last counted through in order) at most 2 rows name the same one
- expert_weights: float32 [2, 256, 4, 8], P('pool', 'ep'), may hold values from 0.1 to 0.6
- gate_w: bfloat16 [128, 3584, 1024], P('ep', None, 'pool'), may hold values from -0.09375 to 0.09375
- up_w: bfloat16 [128, 3584, 1024], P('ep', None, 'pool'), may hold values from -0.09375 to 0.09375
- down_w: bfloat16 [128, 1024, 3584], P('ep', 'pool'), may hold values from -0.1875 to 0.1875
Outputs:
- context: bfloat16 [2, 256, 4, 64, 512], P('pool', 'ep')
- moe_out: bfloat16 [2, 256, 4, 3584], P('pool', 'ep')
Inputs may be any that keep to these rules, and one draw needn't show every extreme that they name: `cache`: the first 512 entries of a row are stored values of a block-scaled format; the last 64 are plain keys. Each group's lengths sum to 10922 and one request has exactly 128. `assign`: each group's row is a permutation of the slots; slot v belongs to ep index v // 2. `expert_ids`: each token names 8 different experts. Within the rows of one device (aligned blocks of 8 tokens in the order group, slot, step) no expert is named more than 2 times, a bound that some block reaches.
All inputs are finite; a program needn't handle non-finite values.
Results may differ from a plain program's by a relative error of at most 0.0057.
Values may be sent and summed in bfloat16 or wider, within the bound.
No kernel may reach another device: no remote copies, remote signals or barrier semaphores. Data moves between devices by JAX's collectives and lax.ppermute only.
A program may use at most 128 MiB of HBM per device.

v0:
```python
import jax
import jax.numpy as jnp
from jax import lax
from jax.sharding import PartitionSpec as P

STEPS = 4
LAT = 512
QB = 128
D = 3584
TOP = 8
EXP_DEV = 1


SCORE_SCALE = 192.0 ** (-0.5)
NEGATIVE = -1e30


def from_partner(block, axis, apart):
    count = lax.axis_size(axis)
    route = []
    for low in range(count):
        high = low | 1 << apart
        if high != low and high < count:
            route += [(low, high), (high, low)]
    return lax.ppermute(block, axis, route)


def half_expert(rows, gate_part, up_part, down_part):
    gate_val = jnp.dot(rows, gate_part, preferred_element_type=jnp.float32)
    up_val = jnp.dot(rows, up_part, preferred_element_type=jnp.float32)
    inner = (jax.nn.silu(gate_val) * up_val).astype(jnp.bfloat16)
    return jnp.dot(inner, down_part, preferred_element_type=jnp.float32)


def on_device(
    cache,
    cache_scale,
    lengths,
    assign,
    queries,
    new_kv,
    hidden,
    expert_ids,
    expert_weights,
    gate_w,
    up_w,
    down_w,
):
    devices = lax.axis_size("ep")
    group_self = lax.axis_index("pool")
    group_other = 1 - group_self
    ep_index = lax.axis_index("ep")
    slot_dev = queries.shape[1]
    head_count = queries.shape[3]
    blocks = LAT // QB
    row_self = lax.dynamic_index_in_dim(assign, group_self, 0, keepdims=False)
    row_other = lax.dynamic_index_in_dim(assign, group_other, 0, keepdims=False)
    pair = (cache[0], cache_scale[0])
    arrived = from_partner(
        (
            lax.all_to_all(
                jnp.zeros_like(pair[0]).at[row_self].set(pair[0]),
                "ep",
                split_axis=0,
                concat_axis=1,
                tiled=True,
            ),
            lax.all_to_all(
                jnp.zeros_like(pair[1]).at[row_self].set(pair[1]),
                "ep",
                split_axis=0,
                concat_axis=1,
                tiled=True,
            ),
        ),
        "pool",
        0,
    )
    rows_cache, rows_scale = arrived
    positions = rows_cache.shape[1]
    length_other = lax.dynamic_index_in_dim(lengths, group_other, 0, keepdims=False)
    slot_length = jnp.zeros(length_other.shape, jnp.int32).at[row_other].set(length_other)
    my_length = lax.dynamic_slice_in_dim(slot_length, ep_index * slot_dev, slot_dev)
    query_rows = queries[0]
    fresh_keys = new_kv[0]
    query_latent = query_rows[..., :LAT].reshape(slot_dev, STEPS, head_count, blocks, QB)
    value_latent = rows_cache[..., :LAT].reshape(slot_dev, positions, blocks, QB)
    scale_full = rows_scale.astype(jnp.float32)
    partial_value = jnp.einsum(
        "bshnc,bpnc->bshpn", query_latent, value_latent, preferred_element_type=jnp.float32
    )
    score_cache = jnp.sum(partial_value * scale_full[:, None, None, :, :], axis=-1)
    score_cache = score_cache + jnp.einsum(
        "bshr,bpr->bshp",
        query_rows[..., LAT:],
        rows_cache[..., LAT:],
        preferred_element_type=jnp.float32,
    )
    score_cache = score_cache * SCORE_SCALE
    position = jnp.arange(positions, dtype=jnp.int32)
    score_cache = jnp.where(
        position[None, None, None, :] < my_length[:, None, None, None], score_cache, NEGATIVE
    )
    score_fresh = (
        jnp.einsum("bshc,btc->bsht", query_rows, fresh_keys, preferred_element_type=jnp.float32)
        * SCORE_SCALE
    )
    step_index = jnp.arange(STEPS, dtype=jnp.int32)
    allowed = step_index[None, None, :] <= step_index[:, None, None]
    score_fresh = jnp.where(allowed[None], score_fresh, NEGATIVE)
    row_max = jnp.maximum(jnp.max(score_cache, axis=-1), jnp.max(score_fresh, axis=-1))[..., None]
    exp_cache = jnp.exp(score_cache - row_max)
    exp_fresh = jnp.exp(score_fresh - row_max)
    summed = jnp.sum(exp_cache, axis=-1, keepdims=True) + jnp.sum(exp_fresh, axis=-1, keepdims=True)
    weight_cache = ((exp_cache / summed)[..., None] * scale_full[:, None, None, :, :]).astype(
        jnp.bfloat16
    )
    weight_fresh = (exp_fresh / summed).astype(jnp.bfloat16)
    latent = jnp.einsum(
        "bshpn,bpnc->bshnc", weight_cache, value_latent, preferred_element_type=jnp.float32
    )
    latent = latent.reshape(slot_dev, STEPS, head_count, LAT)
    latent = latent + jnp.einsum(
        "bsht,btc->bshc", weight_fresh, fresh_keys[..., :LAT], preferred_element_type=jnp.float32
    )
    context = latent.astype(jnp.bfloat16)[None]
    token_count = slot_dev * STEPS
    flat_tokens = hidden[0].reshape(token_count, D)
    expert_list = expert_ids[0].reshape(-1)
    route_weight = expert_weights[0].reshape(-1)
    experts = EXP_DEV * devices
    capacity = max(2, 2 * token_count * TOP // experts)
    owner_token = jnp.arange(token_count * TOP, dtype=jnp.int32) // TOP
    onehot = (expert_list[:, None] == jnp.arange(experts, dtype=jnp.int32)[None, :]).astype(
        jnp.int32
    )
    slot_rank = jnp.sum((jnp.cumsum(onehot, axis=0) - 1) * onehot, axis=1)
    slot_index = expert_list * capacity + slot_rank
    outgoing = (
        jnp.zeros((experts * capacity, D), jnp.bfloat16)
        .at[slot_index]
        .set(flat_tokens[owner_token])
    )
    outgoing = outgoing.reshape(devices, EXP_DEV * capacity, D)
    partner = from_partner((gate_w, up_w, down_w), "pool", 0)
    rows = lax.all_to_all(outgoing, "ep", split_axis=0, concat_axis=0, tiled=True)
    flat_rows = rows.reshape(-1, D)
    result = half_expert(flat_rows, gate_w[0], up_w[0], down_w[0])
    result = result + half_expert(flat_rows, partner[0][0], partner[1][0], partner[2][0])
    served = result.astype(jnp.bfloat16).reshape(rows.shape)
    returned = lax.all_to_all(served, "ep", split_axis=0, concat_axis=0, tiled=True).reshape(
        experts * capacity, D
    )
    picked = returned[slot_index].astype(jnp.float32) * route_weight[:, None]
    combined = jnp.sum(picked.reshape(token_count, TOP, D), axis=1)
    moe_out = combined.astype(jnp.bfloat16).reshape(1, slot_dev, STEPS, D)
    return (context, moe_out)


def solution(mesh):
    return jax.shard_map(
        on_device,
        mesh=mesh,
        in_specs=(
            P("pool", None, "ep", None),
            P("pool", None, "ep", None),
            P(),
            P(),
            P("pool", "ep", None, None, None),
            P("pool", "ep", None, None),
            P("pool", "ep", None, None),
            P("pool", "ep", None, None),
            P("pool", "ep", None, None),
            P("ep", None, "pool"),
            P("ep", None, "pool"),
            P("ep", "pool", None),
        ),
        out_specs=(P("pool", "ep", None, None, None), P("pool", "ep", None, None)),
        check_vma=False,
    )
```

profile of v0, /device:TPU:1, one launch (start us, length us, event | category | flops | bytes accessed | tf_op | source)
XLA Modules:
  0.0 377.1 jit_solution(4515610868125051162)
XLA Ops:
  3.4 3.3 scatter_custom_fusion.3
  6.7 1.7 reshape.228
  8.4 16.5 %all-to-all-start.2 = ((bf16[128,2,3584]{2,1,0:T(2,128)(2,1)}), bf16[128,2,3584]{2,1,0:T(2,128)(2,1)S(1)}, u32[]{:S(2)}, u32[]{:S(2)}) async-start(bf16[128,2,3584]{2,1,0:T(2,128)(2,1)} %reshape.228), calls=%async_computation.2 | async-start | bytes 3670016 | tf_op jit(solution)/shard_map/all_to_all | solution.py:146
  27.0 1.7 scatter_custom_fusion
  33.0 38.9 %all-to-all-done.2 = bf16[128,2,3584]{2,1,0:T(2,128)(2,1)S(1)} async-done(((bf16[128,2,3584]{2,1,0:T(2,128)(2,1)}), bf16[128,2,3584]{2,1,0:T(2,128)(2,1)S(1)}, u32[]{:S(2)}, u32[]{:S(2)}) %all-to-all-start.2) | async-done | bytes 1835040 | tf_op jit(solution)/shard_map/all_to_all | solution.py:146
  71.9 1.2 copy-done.1
  73.1 7.8 %all-to-all-start.1 = ((bf16[256,1,4]{2,1,0:T(2,128)(2,1)}), bf16[256,1,4]{2,1,0:T(2,128)(2,1)S(1)}, u32[]{:S(2)}, u32[]{:S(2)}) async-start(bf16[256,1,4]{2,1,0:T(2,128)(2,1)} %copy.38), calls=%async_computation.1 | async-start | bytes 262144 | tf_op jit(solution)/shard_map/all_to_all | solution.py:68
  80.9 4.1 %reshape.229 = bf16[256,3584]{1,0:T(8,128)(2,1)S(1)} reshape(bf16[128,2,3584]{2,1,0:T(2,128)(2,1)} %copy-done.1) | data formatting | bytes 3670016 | tf_op jit(solution)/shard_map/reshape | solution.py:147
  85.0 3.1 fusion.10
  88.1 7.2 %fusion.6 = f32[256,3584]{1,0:T(8,128)} fusion(bf16[1,512,3584]{2,1,0:T(8,128)(2,1)} %param.23, bf16[256,3584]{1,0:T(8,128)(2,1)S(1)} %reshape.229, bf16[1,3584,512]{2,1,0:T(8,128)(2,1)} %param.22, f32[256,512]{1,0:T(8,128)S(1)} %fusion.10), kind=kOutput, calls=%fused_computation.13 | convolution fusion | flops 1879834624 | bytes 13369344 | tf_op jit(solution)/shard_map/dot_general | solution.py:32
  95.4 29.8 %collective-permute-done.3 = bf16[1,3584,512]{2,1,0:T(8,128)(2,1)} collective-permute-done((bf16[1,3584,512]{2,1,0:T(8,128)(2,1)}, bf16[1,3584,512]{2,1,0:T(8,128)(2,1)}, u32[]{:S(2)}, u32[]{:S(2)}) %collective-permute-start.3) | collective-permute-done | bytes 3670048 | tf_op jit(solution)/shard_map/ppermute | solution.py:25
  125.1 3.1 fusion.2
  128.3 160.1 %all-to-all-done.1 = bf16[256,1,4]{2,1,0:T(2,128)(2,1)S(1)} async-done(((bf16[256,1,4]{2,1,0:T(2,128)(2,1)}), bf16[256,1,4]{2,1,0:T(2,128)(2,1)S(1)}, u32[]{:S(2)}, u32[]{:S(2)}) %all-to-all-start.1) | async-done | bytes 2080 | tf_op jit(solution)/shard_map/all_to_all | solution.py:68
  288.4 9.1 %all-to-all-start = ((bf16[128,2,576]{2,1,0:T(2,128)(2,1)}), bf16[128,2,576]{2,1,0:T(2,128)(2,1)S(1)}, u32[]{:S(2)}, u32[]{:S(2)}) async-start(bf16[128,2,576]{2,1,0:T(2,128)(2,1)} %reshape.306), calls=%async_computation | async-start | bytes 655360 | tf_op jit(solution)/shard_map/all_to_all | solution.py:61
  297.6 7.8 %fusion = bf16[256,3584]{1,0:T(8,128)(2,1)} fusion(f32[256,3584]{1,0:T(8,128)} %fusion.6, bf16[1,512,3584]{2,1,0:T(8,128)(2,1)} %collective-permute-done.4, f32[256,512]{1,0:T(8,128)S(1)} %fusion.2, bf16[256,3584]{1,0:T(8,128)(2,1)S(1)} %reshape.229, bf16[1,3584,512]{2,1,0:T(8,128)(2,1)} %collective-permute-done.2), kind=kOutput, calls=%fused_computation.7 | convolution fusion | flops 1881669632 | bytes 15204352 | tf_op jit(solution)/shard_map/dot_general | solution.py:32
  305.3 4.9 %reshape.230 = bf16[128,2,3584]{2,1,0:T(2,128)(2,1)} reshape(bf16[256,3584]{1,0:T(8,128)(2,1)} %fusion) | data formatting | bytes 3670016 | tf_op jit(solution)/shard_map/reshape | solution.py:150
  310.2 4.8 %all-to-all-done = bf16[128,2,576]{2,1,0:T(2,128)(2,1)S(1)} async-done(((bf16[128,2,576]{2,1,0:T(2,128)(2,1)}), bf16[128,2,576]{2,1,0:T(2,128)(2,1)S(1)}, u32[]{:S(2)}, u32[]{:S(2)}) %all-to-all-start) | async-done | bytes 294944 | tf_op jit(solution)/shard_map/all_to_all | solution.py:61
  315.0 9.4 %all-to-all-start.3 = ((bf16[128,2,3584]{2,1,0:T(2,128)(2,1)}), bf16[128,2,3584]{2,1,0:T(2,128)(2,1)}, u32[]{:S(2)}, u32[]{:S(2)}) async-start(bf16[128,2,3584]{2,1,0:T(2,128)(2,1)} %reshape.230), calls=%async_computation.3 | async-start | bytes 3670016 | tf_op jit(solution)/shard_map/all_to_all | solution.py:151
  324.5 1.6 scatter_custom_fusion.1
  327.1 2.2 reduce
  330.8 1.2 collective-permute-start.1
  332.0 10.2 %collective-permute-done.1 = bf16[2,128,4]{1,2,0:T(4,128)(2,1)S(1)} collective-permute-done((bf16[2,128,4]{1,2,0:T(4,128)(2,1)S(1)}, bf16[2,128,4]{1,2,0:T(4,128)(2,1)S(1)}, u32[]{:S(2)}, u32[]{:S(2)}) %collective-permute-start.1) | collective-permute-done | bytes 2080 | tf_op jit(solution)/shard_map/ppermute | solution.py:25
  344.9 26.2 %all-to-all-done.3 = bf16[128,2,3584]{2,1,0:T(2,128)(2,1)} async-done(((bf16[128,2,3584]{2,1,0:T(2,128)(2,1)}), bf16[128,2,3584]{2,1,0:T(2,128)(2,1)}, u32[]{:S(2)}, u32[]{:S(2)}) %all-to-all-start.3) | async-done | bytes 1835040 | tf_op jit(solution)/shard_map/all_to_all | solution.py:151
  371.1 4.1 %reshape.231 = bf16[256,3584]{1,0:T(8,128)(2,1)S(1)} reshape(bf16[128,2,3584]{2,1,0:T(2,128)(2,1)} %all-to-all-done.3) | data formatting | bytes 3670016 | tf_op jit(solution)/shard_map/reshape | solution.py:151
  (66 shorter events, 16.1 us)
Async XLA Ops:
  0.6 323.8 %copy-start = (s32[2,256]{1,0:T(2,128)S(1)}, s32[2,256]{1,0:T(2,128)}, u32[]{:S(2)}) copy-start(s32[2,256]{1,0:T(2,128)} %param.14) | copy-start | bytes 6148
  6.7 20.1 %copy-start.3 = (bf16[1,256,1,576]{1,3,2,0:T(8,128)(2,1)S(1)}, bf16[1,256,1,576]{1,3,2,0:T(8,128)(2,1)}, u32[]{:S(2)}) copy-start(bf16[1,256,1,576]{1,3,2,0:T(8,128)(2,1)} %param.12) | copy-start | bytes 884740
  6.7 20.3 %copy-start.7 = (s32[2,256]{1,0:T(2,128)S(1)}, s32[2,256]{1,0:T(2,128)}, u32[]{:S(2)}) copy-start(s32[2,256]{1,0:T(2,128)} %param.15) | copy-start | bytes 6148
  8.4 22.5 %copy-start.6 = (bf16[1,256,1,4]{1,3,2,0:T(4,128)(2,1)S(1)}, bf16[1,256,1,4]{1,3,2,0:T(4,128)(2,1)}, u32[]{:S(2)}) copy-start(bf16[1,256,1,4]{1,3,2,0:T(4,128)(2,1)} %param.13) | copy-start | bytes 6148
  8.4 63.5 %all-to-all-start.2 = ((bf16[128,2,3584]{2,1,0:T(2,128)(2,1)}), bf16[128,2,3584]{2,1,0:T(2,128)(2,1)S(1)}, u32[]{:S(2)}, u32[]{:S(2)}) async-start(bf16[128,2,3584]{2,1,0:T(2,128)(2,1)} %reshape.228), calls=%async_computation.2 | async-start | bytes 3670016 | tf_op jit(solution)/shard_map/all_to_all | solution.py:146
  24.9 100.2 %collective-permute-start.3 = (bf16[1,3584,512]{2,1,0:T(8,128)(2,1)}, bf16[1,3584,512]{2,1,0:T(8,128)(2,1)}, u32[]{:S(2)}, u32[]{:S(2)}) collective-permute-start(bf16[1,3584,512]{2,1,0:T(8,128)(2,1)} %param.22), channel_id=1, source_target_pairs={{0,128},{128,0},{1,129},{129,1},{2,130},{130,2},{3,131},{131,3},{4... | collective-permute-start | bytes 11010056 | tf_op jit(solution)/shard_map/ppermute | solution.py:25
  25.3 272.2 %collective-permute-start.2 = (bf16[1,3584,512]{2,1,0:T(8,128)(2,1)}, bf16[1,3584,512]{2,1,0:T(8,128)(2,1)}, u32[]{:S(2)}, u32[]{:S(2)}) collective-permute-start(bf16[1,3584,512]{2,1,0:T(8,128)(2,1)} %param.21), channel_id=1, source_target_pairs={{0,128},{128,0},{1,129},{129,1},{2,130},{130,2},{3,131},{131,3},{4... | collective-permute-start | bytes 11010056 | tf_op jit(solution)/shard_map/ppermute | solution.py:25
  26.5 271.1 %collective-permute-start.4 = (bf16[1,512,3584]{2,1,0:T(8,128)(2,1)}, bf16[1,512,3584]{2,1,0:T(8,128)(2,1)}, u32[]{:S(2)}, u32[]{:S(2)}) collective-permute-start(bf16[1,512,3584]{2,1,0:T(8,128)(2,1)} %param.23), channel_id=1, source_target_pairs={{0,128},{128,0},{1,129},{129,1},{2,130},{130,2},{3,131},{131,3},{4... | collective-permute-start | bytes 11010056 | tf_op jit(solution)/shard_map/ppermute | solution.py:25
  71.9 1.2 copy-start.1
  73.1 215.3 %all-to-all-start.1 = ((bf16[256,1,4]{2,1,0:T(2,128)(2,1)}), bf16[256,1,4]{2,1,0:T(2,128)(2,1)S(1)}, u32[]{:S(2)}, u32[]{:S(2)}) async-start(bf16[256,1,4]{2,1,0:T(2,128)(2,1)} %copy.38), calls=%async_computation.1 | async-start | bytes 262144 | tf_op jit(solution)/shard_map/all_to_all | solution.py:68
  288.4 26.6 %all-to-all-start = ((bf16[128,2,576]{2,1,0:T(2,128)(2,1)}), bf16[128,2,576]{2,1,0:T(2,128)(2,1)S(1)}, u32[]{:S(2)}, u32[]{:S(2)}) async-start(bf16[128,2,576]{2,1,0:T(2,128)(2,1)} %reshape.306), calls=%async_computation | async-start | bytes 655360 | tf_op jit(solution)/shard_map/all_to_all | solution.py:61
  305.3 20.9 %copy-start.2 = (bf16[1,2,4,64,576]{4,3,2,1,0:T(8,128)(2,1)S(1)}, bf16[1,2,4,64,576]{4,3,2,1,0:T(8,128)(2,1)}, u32[]{:S(2)}) copy-start(bf16[1,2,4,64,576]{4,3,2,1,0:T(8,128)(2,1)} %param.16) | copy-start | bytes 1769476
  305.3 20.9 %copy-start.4 = (bf16[1,2,4,576]{3,2,1,0:T(4,128)(2,1)S(1)}, bf16[1,2,4,576]{3,2,1,0:T(4,128)(2,1)}, u32[]{:S(2)}) copy-start(bf16[1,2,4,576]{3,2,1,0:T(4,128)(2,1)} %param.17) | copy-start | bytes 27652
  315.0 56.1 %all-to-all-start.3 = ((bf16[128,2,3584]{2,1,0:T(2,128)(2,1)}), bf16[128,2,3584]{2,1,0:T(2,128)(2,1)}, u32[]{:S(2)}, u32[]{:S(2)}) async-start(bf16[128,2,3584]{2,1,0:T(2,128)(2,1)} %reshape.230), calls=%async_computation.3 | async-start | bytes 3670016 | tf_op jit(solution)/shard_map/all_to_all | solution.py:151
  330.2 12.0 %collective-permute-start = (bf16[2,128,576]{1,2,0:T(8,128)(2,1)S(1)}, bf16[2,128,576]{1,2,0:T(8,128)(2,1)S(1)}, u32[]{:S(2)}, u32[]{:S(2)}) collective-permute-start(bf16[2,128,576]{1,2,0:T(8,128)(2,1)S(1)} %bitcast.129), channel_id=1, source_target_pairs={{0,128},{128,0},{1,129},{129,1},{2,130},{130,2},{3,131},{131,3},{4... | collective-permute-start | bytes 884744 | tf_op jit(solution)/shard_map/ppermute | solution.py:25
  330.8 11.4 %collective-permute-start.1 = (bf16[2,128,4]{1,2,0:T(4,128)(2,1)S(1)}, bf16[2,128,4]{1,2,0:T(4,128)(2,1)S(1)}, u32[]{:S(2)}, u32[]{:S(2)}) collective-permute-start(bf16[2,128,4]{1,2,0:T(4,128)(2,1)S(1)} %bitcast.135), channel_id=1, source_target_pairs={{0,128},{128,0},{1,129},{129,1},{2,130},{130,2},{3,131},{131,3},{4... | collective-permute-start | bytes 6152 | tf_op jit(solution)/shard_map/ppermute | solution.py:25
  344.9 31.1 %copy-start.5 = (f32[1,2,4,8]{3,2,1,0:T(4,128)S(1)}, f32[1,2,4,8]{3,2,1,0:T(4,128)}, u32[]{:S(2)}) copy-start(f32[1,2,4,8]{3,2,1,0:T(4,128)} %param.20) | copy-start | bytes 772
where the time goes:
time: 379 us; the launch traced here: 377 us
  waiting for transfers between devices  270 us (71%)
  starting transfers between devices  46.3 us (12%)
  local copies, waits for them, and re-layouts  30.9 us (8%)
  matrix products  23.7 us (6%)
  other arithmetic  5.16 us (1%)
    all_to_all x1, waiting for transfers between devices, on_device(): lax.all_to_all(jnp.zeros_like(pair[1]).at[row_self].set(pair[1]), 'ep', s...  160 us
    ppermute x5, waiting for transfers between devices, from_partner(): return lax.ppermute(block, axis, route)  40 us
    all_to_all x1, waiting for transfers between devices, on_device(): lax.all_to_all(outgoing, 'ep', split_axis=0, concat_axis=0, tiled=True)  38.9 us
    all_to_all x1, waiting for transfers between devices, on_device(): lax.all_to_all(served, 'ep', split_axis=0, concat_axis=0, tiled=True)  26.2 us
    all_to_all x1, starting transfers between devices, on_device(): lax.all_to_all(outgoing, 'ep', split_axis=0, concat_axis=0, tiled=True)  16.5 us
    dot_general x2, matrix products, half_expert(): return jnp.dot(inner, down_part, preferred_element_type=jnp.float32)  15 us
    all_to_all x1, starting transfers between devices, on_device(): lax.all_to_all(served, 'ep', split_axis=0, concat_axis=0, tiled=True)  9.41 us
    all_to_all x1, starting transfers between devices, on_device(): lax.all_to_all(jnp.zeros_like(pair[0]).at[row_self].set(pair[0]), 'ep', s...  9.14 us
  transfers between devices with their start and end apart: 9, of which 6 were waited for; matrix products, arithmetic and copies ran while one was open for 12% of the time, Pallas kernels for 0%

commit v1 on v0

v1 whole, which is shorter than its diff:
```python
import jax
import jax.numpy as jnp
from jax import lax
from jax.sharding import Mesh, PartitionSpec as P

STEPS = 4
LAT = 512
ROPE = 64
QB = 128
D = 3584
TOP = 8
CAP = 2

Y, XH, Z, CORE = 4, 2, 8, 2
PLANE = Y * XH
LINE = Z * CORE
KEEP = LINE * CAP

SCORE_SCALE = 192.0 ** (-0.5)
NEGATIVE = -1e30

LINE_AXES = ("z", "core")
PLANE_AXES = ("y", "xh")
CROSS_AXES = ("pool", "y", "xh")
EP_AXES = ("y", "xh", "z", "core")


def narrowed(value):
    return lax.reduce_precision(value, 8, 7)


def pieces(value):
    first = narrowed(value)
    rest = value - first
    second = narrowed(rest)
    return [part.astype(jnp.bfloat16) for part in (first, second, rest - second)]


def exact_rows(choose, rows):
    return jnp.dot(choose, rows, preferred_element_type=jnp.float32).astype(jnp.bfloat16)


def attend(latent_rows, rope_rows, scale_rows, lengths, query_rows, fresh_keys):
    slot_dev, positions = latent_rows.shape[:2]
    head_count = query_rows.shape[2]
    blocks = LAT // QB
    query_latent = query_rows[..., :LAT].reshape(slot_dev, STEPS, head_count, blocks, QB)
    value_latent = latent_rows.reshape(slot_dev, positions, blocks, QB)
    scale_full = scale_rows.astype(jnp.float32)
    partial_value = jnp.einsum(
        "bshnc,bpnc->bshpn", query_latent, value_latent, preferred_element_type=jnp.float32
    )
    score_cache = jnp.sum(partial_value * scale_full[:, None, None, :, :], axis=-1)
    score_cache = score_cache + jnp.einsum(
        "bshr,bpr->bshp", query_rows[..., LAT:], rope_rows, preferred_element_type=jnp.float32
    )
    score_cache = score_cache * SCORE_SCALE
    position = jnp.arange(positions, dtype=jnp.int32)
    score_cache = jnp.where(
        position[None, None, None, :] < lengths[:, None, None, None], score_cache, NEGATIVE
    )
    score_fresh = (
        jnp.einsum("bshc,btc->bsht", query_rows, fresh_keys, preferred_element_type=jnp.float32)
        * SCORE_SCALE
    )
    step_index = jnp.arange(STEPS, dtype=jnp.int32)
    allowed = step_index[None, None, :] <= step_index[:, None, None]
    score_fresh = jnp.where(allowed[None], score_fresh, NEGATIVE)
    row_max = jnp.maximum(jnp.max(score_cache, axis=-1), jnp.max(score_fresh, axis=-1))[..., None]
    exp_cache = jnp.exp(score_cache - row_max)
    exp_fresh = jnp.exp(score_fresh - row_max)
    summed = jnp.sum(exp_cache, axis=-1, keepdims=True) + jnp.sum(exp_fresh, axis=-1, keepdims=True)
    weight_cache = ((exp_cache / summed)[..., None] * scale_full[:, None, None, :, :]).astype(
        jnp.bfloat16
    )
    weight_fresh = (exp_fresh / summed).astype(jnp.bfloat16)
    latent = jnp.einsum(
        "bshpn,bpnc->bshnc", weight_cache, value_latent, preferred_element_type=jnp.float32
    )
    latent = latent.reshape(slot_dev, STEPS, head_count, LAT)
    latent = latent + jnp.einsum(
        "bsht,btc->bshc", weight_fresh, fresh_keys[..., :LAT], preferred_element_type=jnp.float32
    )
    return latent.astype(jnp.bfloat16)[None]


def on_device(
    cache,
    cache_scale,
    lengths,
    assign,
    queries,
    new_kv,
    hidden,
    expert_ids,
    expert_weights,
    gate_w,
    up_w,
    down_w,
):
    group_self = lax.axis_index("pool")
    yx_self = lax.axis_index(PLANE_AXES)
    zc_self = lax.axis_index(LINE_AXES)
    slot_dev = queries.shape[1]
    slots = assign.shape[1]
    token_count = slot_dev * STEPS
    line_tokens = LINE * token_count

    ids = expert_ids[0].reshape(token_count, TOP).astype(jnp.bfloat16)
    weights = expert_weights[0].reshape(token_count, TOP)
    routing = jnp.concatenate([ids] + pieces(weights), axis=1)
    routing = jnp.pad(routing, ((0, 0), (0, 128 - 4 * TOP)))
    token_rows = jnp.concatenate([hidden[0].reshape(token_count, D), routing], axis=1)
    line = lax.all_gather(token_rows, LINE_AXES, axis=0, tiled=True)

    row_self = lax.dynamic_index_in_dim(assign, group_self, 0, keepdims=False)
    place = jnp.arange(slots, dtype=jnp.int32)
    slot_at = (place // slot_dev % PLANE) * (LINE * slot_dev) + (
        place // (slot_dev * PLANE)
    ) * slot_dev + place % slot_dev
    by_slot = (row_self[None, :] == slot_at[:, None]).astype(jnp.bfloat16)
    stored = jnp.concatenate([cache[0, :, 0, :], cache_scale[0, :, 0, :]], axis=1)
    stored = jnp.pad(stored, ((0, 0), (0, 640 - stored.shape[1])))
    outbound = lax.ppermute(exact_rows(by_slot, stored), "pool", [(0, 1), (1, 0)])
    along = lax.all_to_all(
        outbound.reshape(LINE, PLANE * slot_dev, 640), LINE_AXES, 0, 0, tiled=True
    ).reshape(slots, 640)
    wanted = (place % LINE) * (PLANE * slot_dev) + (
        place // (LINE * slot_dev)
    ) * slot_dev + place // LINE % slot_dev
    shuffle = (place[None, :] == wanted[:, None]).astype(jnp.bfloat16)
    across = lax.all_to_all(
        exact_rows(shuffle, along).reshape(PLANE, slot_dev * LINE, 640), PLANE_AXES, 0, 0, tiled=True
    ).reshape(PLANE, slot_dev, LINE, 640)
    slot_rows = jnp.swapaxes(across, 0, 1).reshape(slot_dev, PLANE * LINE, 640)

    length_other = lax.dynamic_index_in_dim(lengths, 1 - group_self, 0, keepdims=False)
    row_other = lax.dynamic_index_in_dim(assign, 1 - group_self, 0, keepdims=False)
    my_slots = (yx_self * LINE + zc_self) * slot_dev + jnp.arange(slot_dev, dtype=jnp.int32)
    my_length = jnp.sum(
        jnp.where(row_other[None, :] == my_slots[:, None], length_other[None, :], 0), axis=1
    )

    line_ids = line[:, D : D + TOP].astype(jnp.int32)
    line_weights = sum(
        line[:, D + TOP * part : D + TOP * (part + 1)].astype(jnp.float32) for part in (1, 2, 3)
    )
    experts = jnp.arange(PLANE, dtype=jnp.int32) * LINE + zc_self
    named = line_ids[None, :, :] == experts[:, None, None]
    hit = jnp.any(named, axis=2)
    weight_of = jnp.sum(jnp.where(named, line_weights[None], 0.0), axis=2)
    earlier = (
        jnp.arange(line_tokens)[:, None] < jnp.arange(line_tokens)[None, :]
    ).astype(jnp.bfloat16)
    rank = jnp.dot(
        hit.astype(jnp.bfloat16), earlier, preferred_element_type=jnp.float32
    ).astype(jnp.int32)
    rank = jnp.where(hit, rank, -1)
    chosen = rank[:, None, :] == jnp.arange(KEEP, dtype=jnp.int32)[None, :, None]
    choose = chosen.astype(jnp.bfloat16).reshape(PLANE * KEEP, line_tokens)
    rows = exact_rows(choose, line[:, :D])
    sent = jnp.concatenate([rows, rows], axis=0).reshape(2 * PLANE, KEEP, D)
    taken = lax.all_to_all(sent, CROSS_AXES, 0, 0, tiled=True).reshape(2 * PLANE * KEEP, D)

    gate_val = jnp.dot(taken, gate_w[0], preferred_element_type=jnp.float32)
    up_val = jnp.dot(taken, up_w[0], preferred_element_type=jnp.float32)
    inner = (jax.nn.silu(gate_val) * up_val).astype(jnp.bfloat16)
    served = jnp.dot(inner, down_w[0], preferred_element_type=jnp.float32).astype(jnp.bfloat16)
    back = lax.all_to_all(
        served.reshape(2 * PLANE, KEEP, D), CROSS_AXES, 0, 0, tiled=True
    ).reshape(2 * PLANE * KEEP, D)

    mix = jnp.where(chosen, weight_of[:, None, :], 0.0).reshape(PLANE * KEEP, line_tokens).T
    mix_high = narrowed(mix)
    mix_parts = [part.astype(jnp.bfloat16) for part in (mix_high, mix - mix_high)]
    mixed = sum(
        jnp.dot(jnp.concatenate([part, part], axis=1), back, preferred_element_type=jnp.float32)
        for part in mix_parts
    ).astype(jnp.bfloat16)
    gathered = lax.all_to_all(
        mixed.reshape(LINE, token_count, D), LINE_AXES, 0, 0, tiled=True
    )
    moe_out = jnp.sum(gathered.astype(jnp.float32), axis=0).astype(jnp.bfloat16)

    context = attend(
        slot_rows[..., :LAT],
        slot_rows[..., LAT : LAT + ROPE],
        slot_rows[..., LAT + ROPE : LAT + ROPE + LAT // QB],
        my_length,
        queries[0],
        new_kv[0],
    )
    return (context, moe_out.reshape(1, slot_dev, STEPS, D))


def solution(mesh):
    fine = Mesh(
        mesh.devices.reshape(2, Y, XH, Z, CORE), ("pool", "y", "xh", "z", "core")
    )
    return jax.shard_map(
        on_device,
        mesh=fine,
        in_specs=(
            P("pool", None, EP_AXES, None),
            P("pool", None, EP_AXES, None),
            P(),
            P(),
            P("pool", EP_AXES, None, None, None),
            P("pool", EP_AXES, None, None),
            P("pool", EP_AXES, None, None),
            P("pool", EP_AXES, None, None),
            P("pool", EP_AXES, None, None),
            P(EP_AXES, None, "pool"),
            P(EP_AXES, None, "pool"),
            P(EP_AXES, "pool", None),
        ),
        out_specs=(P("pool", EP_AXES, None, None, None), P("pool", EP_AXES, None, None)),
        check_vma=False,
    )
```

time: 379 us -> 242 us (0.64)
  waiting for transfers between devices: 270 us -> 148 us
  local copies, waits for them, and re-layouts: 30.9 us -> 2.49 us
  blocking collectives: 0 us -> 23.9 us
  starting transfers between devices: 46.3 us -> 33.9 us
    all_to_all x4 -> x5, waiting for transfers between devices: 230 us -> 81.5 us  [the longest x1 58 us: on_device(): lax.all_to_all(served.reshape(2 * PLANE, KEEP, D), CROSS_AXES, 0, 0, tile...]
    ppermute x5 -> x1, waiting for transfers between devices: 40 us -> 66.6 us  [on_device(): lax.ppermute(exact_rows(by_slot, stored), 'pool', [(0, 1), (1, 0)])]
    all_gather x0 -> x1, blocking collectives: none -> 23.9 us  [on_device(): line = lax.all_gather(token_rows, LINE_AXES, axis=0, tiled=True)]
    reshape x5 -> x2, local copies, waits for them, and re-layouts: 14.8 us -> 0.77 us  [the longest x1 0.64 us: on_device(): return (context, moe_out.reshape(1, slot_dev, STEPS, D))]
    all_to_all x4 -> x5, starting transfers between devices: 42.8 us -> 32.5 us  [the longest x1 7.65 us: on_device(): lax.all_to_all(mixed.reshape(LINE, token_count, D), LINE_AXES, 0, 0, tile...]
    scatter x6 -> x0, local copies, waits for them, and re-layouts: 9.01 us -> none  [the longest x1 3.26 us: on_device(): outgoing = jnp.zeros((experts * capacity, D), jnp.bfloat16).at[slot_index...]
    dot_general x8 -> x12, matrix products: 23.5 us -> 26 us  [the longest x1 10.1 us: on_device(): jnp.dot(inner, down_w[0], preferred_element_type=jnp.float32)]
  transfers between devices with their start and end apart: 9 -> 6, of which waited for: 6 -> 4; matrix products, arithmetic and copies ran while one was open for 12% -> 11% of each run, Pallas kernels for 0% -> 0%
where the time goes in v1:
time: 242 us; the launch traced here: 241 us
  waiting for transfers between devices  148 us (61%)
  starting transfers between devices  33.9 us (14%)
  matrix products  26.3 us (11%)
  blocking collectives  23.9 us (10%)
  other arithmetic  5.1 us (2%)
  local copies, waits for them, and re-layouts  2.49 us (1%)
    ppermute x1, waiting for transfers between devices, on_device(): lax.ppermute(exact_rows(by_slot, stored), 'pool', [(0, 1), (1, 0)])  66.6 us
    all_to_all x1, waiting for transfers between devices, on_device(): lax.all_to_all(served.reshape(2 * PLANE, KEEP, D), CROSS_AXES, 0, 0, tile...  58 us
    all_gather x1, blocking collectives, on_device(): line = lax.all_gather(token_rows, LINE_AXES, axis=0, tiled=True)  23.9 us
    all_to_all x1, waiting for transfers between devices, on_device(): lax.all_to_all(mixed.reshape(LINE, token_count, D), LINE_AXES, 0, 0, tile...  21.9 us
    dot_general x1, matrix products, on_device(): jnp.dot(inner, down_w[0], preferred_element_type=jnp.float32)  10.1 us
    all_to_all x1, starting transfers between devices, on_device(): lax.all_to_all(mixed.reshape(LINE, token_count, D), LINE_AXES, 0, 0, tile...  7.65 us
    all_to_all x1, starting transfers between devices, on_device(): lax.all_to_all(sent, CROSS_AXES, 0, 0, tiled=True)  6.94 us
    all_to_all x1, starting transfers between devices, on_device(): lax.all_to_all(exact_rows(shuffle, along).reshape(PLANE, slot_dev * LINE,...  6.8 us
  transfers between devices with their start and end apart: 6, of which 4 were waited for; matrix products, arithmetic and copies ran while one was open for 11% of the time, Pallas kernels for 0%

profile of v1, /device:TPU:1, one launch (start us, length us, event | category | flops | bytes accessed | tf_op | source)
XLA Modules:
  0.0 240.8 jit_solution(17396478278476060117)
XLA Ops:
  0.6 0.7 reduce-precision_convert_fusion.2
  1.3 0.7 convert_element_type.83
  2.0 0.8 reshape_squeeze.7
  2.9 23.9 %all_gather.3 = bf16[128,3712]{1,0:T(8,128)(2,1)S(1)} all-gather(bf16[8,3712]{1,0:T(8,128)(2,1)S(1)} %pad_maximum_fusion.1), channel_id=1, replica_groups=mesh['pool'=2,'y'=4,'xh'=2,'z'=8,'core'=2] {'z','core'}, dimensions={0}, use_global_device_ids=true | all-gather | bytes 1009664 | tf_op jit(solution)/shard_map/all_gather | solution.py:114
  27.5 0.6 convolution_convert_fusion.1
  28.1 2.1 pad_maximum_fusion
  30.3 6.9 %all-to-all-start.2 = ((bf16[16,32,3584]{2,1,0:T(8,128)(2,1)}), bf16[16,32,3584]{2,1,0:T(8,128)(2,1)}, u32[]{:S(2)}, u32[]{:S(2)}) async-start(bf16[16,32,3584]{2,1,0:T(8,128)(2,1)} %bitcast.117), calls=%async_computation.2 | async-start | bytes 7340032 | tf_op jit(solution)/shard_map/all_to_all | solution.py:163
  37.6 1.4 collective-permute-start
  39.0 66.6 %collective-permute-done = bf16[256,640]{1,0:T(8,128)(2,1)} collective-permute-done((bf16[256,640]{1,0:T(8,128)(2,1)S(1)}, bf16[256,640]{1,0:T(8,128)(2,1)}, u32[]{:S(2)}, u32[]{:S(2)}) %collective-permute-start) | collective-permute-done | bytes 327712 | tf_op jit(solution)/shard_map/ppermute | solution.py:124
  105.7 4.9 %all-to-all-start = ((bf16[16,16,640]{2,1,0:T(8,128)(2,1)}), bf16[16,16,640]{2,1,0:T(8,128)(2,1)S(1)}, u32[]{:S(2)}, u32[]{:S(2)}) async-start(bf16[16,16,640]{2,1,0:T(8,128)(2,1)} %bitcast.3), calls=%async_computation | async-start | bytes 655360 | tf_op jit(solution)/shard_map/all_to_all | solution.py:125
  110.6 5.2 %fusion.5 = f32[512,512]{1,0:T(8,128)S(1)} fusion(bf16[512,3584]{1,0:T(8,128)(2,1)} %bitcast.34, bf16[1,3584,512]{2,1,0:T(8,128)(2,1)} %param.21), kind=kOutput, calls=%fused_computation.9 | convolution fusion | flops 1879048192 | bytes 8388608 | tf_op jit(solution)/shard_map/dot_general | solution.py:165
  115.8 10.1 %convolution_convert_fusion = bf16[512,3584]{1,0:T(8,128)(2,1)} fusion(bf16[1,512,3584]{2,1,0:T(8,128)(2,1)} %param.23, bf16[512,3584]{1,0:T(8,128)(2,1)} %bitcast.34, bf16[1,3584,512]{2,1,0:T(8,128)(2,1)} %param.22, f32[512,512]{1,0:T(8,128)S(1)} %fusion.5), kind=kOutput, calls=%fused_computation | convolution fusion | flops 3761504256 | bytes 15728640 | tf_op jit(solution)/shard_map/dot_general | solution.py:168
  125.9 6.2 %all-to-all-start.3 = ((bf16[16,32,3584]{2,1,0:T(8,128)(2,1)}), bf16[16,32,3584]{2,1,0:T(8,128)(2,1)}, u32[]{:S(2)}, u32[]{:S(2)}) async-start(bf16[16,32,3584]{2,1,0:T(8,128)(2,1)} %bitcast.119), calls=%async_computation.3 | async-start | bytes 7340032 | tf_op jit(solution)/shard_map/all_to_all | solution.py:169
  132.8 0.4 fusion.86
  133.2 1.0 convolution_convert_fusion.2
  134.3 58.0 %all-to-all-done.3 = bf16[16,32,3584]{2,1,0:T(8,128)(2,1)} async-done(((bf16[16,32,3584]{2,1,0:T(8,128)(2,1)}), bf16[16,32,3584]{2,1,0:T(8,128)(2,1)}, u32[]{:S(2)}, u32[]{:S(2)}) %all-to-all-start.3) | async-done | bytes 3670048 | tf_op jit(solution)/shard_map/all_to_all | solution.py:169
  192.3 6.8 %all-to-all-start.1 = ((bf16[8,32,640]{2,1,0:T(8,128)(2,1)}), bf16[8,32,640]{2,1,0:T(8,128)(2,1)S(1)}, u32[]{:S(2)}, u32[]{:S(2)}) async-start(bf16[8,32,640]{2,1,0:T(8,128)(2,1)} %bitcast.5), calls=%async_computation.1 | async-start | bytes 655360 | tf_op jit(solution)/shard_map/all_to_all | solution.py:132
  199.1 2.7 %fusion.40 = f32[128,3584]{1,0:T(8,128)S(1)} fusion(bf16[512,3584]{1,0:T(8,128)(2,1)} %bitcast.39, bf16[128,256]{0,1:T(8,128)(2,1)S(1)} %get-tuple-element.7), kind=kOutput, calls=%fused_computation.52 | convolution fusion | flops 470024192 | bytes 5570560 | tf_op jit(solution)/shard_map/dot_general | solution.py:177
  201.8 3.7 %fusion.1 = bf16[16,8,3584]{2,1,0:T(8,128)(2,1)} fusion(f32[128,3584]{1,0:T(8,128)S(1)} %fusion.40, bf16[512,3584]{1,0:T(8,128)(2,1)} %bitcast.39, bf16[128,256]{0,1:T(8,128)(2,1)S(1)} %get-tuple-element.6), kind=kOutput, calls=%fused_computation.4 | convolution fusion | flops 470941696 | bytes 6488064 | tf_op jit(solution)/shard_map/dot_general | solution.py:177
  205.5 1.6 all-to-all-done.1
  207.1 7.7 %all-to-all-start.4 = ((bf16[16,8,3584]{2,1,0:T(8,128)(2,1)}), bf16[16,8,3584]{2,1,0:T(8,128)(2,1)S(1)}, u32[]{:S(2)}, u32[]{:S(2)}) async-start(bf16[16,8,3584]{2,1,0:T(8,128)(2,1)} %fusion.1), calls=%async_computation.4 | async-start | bytes 1835008 | tf_op jit(solution)/shard_map/all_to_all | solution.py:180
  217.0 1.2 fusion.14
  218.1 21.9 %all-to-all-done.4 = bf16[16,8,3584]{2,1,0:T(8,128)(2,1)S(1)} async-done(((bf16[16,8,3584]{2,1,0:T(8,128)(2,1)}), bf16[16,8,3584]{2,1,0:T(8,128)(2,1)S(1)}, u32[]{:S(2)}, u32[]{:S(2)}) %all-to-all-start.4) | async-done | bytes 917536 | tf_op jit(solution)/shard_map/all_to_all | solution.py:180
  240.1 0.6 reshape.206
  (56 shorter events, 4.0 us)
Async XLA Ops:
  30.2 7.0 %copy-start.2 = (s32[2,256]{1,0:T(2,128)S(1)}, s32[2,256]{1,0:T(2,128)}, u32[]{:S(2)}) copy-start(s32[2,256]{1,0:T(2,128)} %param.15) | copy-start | bytes 6148
  30.2 7.0 %copy-start.3 = (s32[2,256]{1,0:T(2,128)S(1)}, s32[2,256]{1,0:T(2,128)}, u32[]{:S(2)}) copy-start(s32[2,256]{1,0:T(2,128)} %param.14) | copy-start | bytes 6148
  30.3 7.0 %copy-start.4 = (bf16[1,256,1,576]{1,3,2,0:T(8,128)(2,1)S(1)}, bf16[1,256,1,576]{1,3,2,0:T(8,128)(2,1)}, u32[]{:S(2)}) copy-start(bf16[1,256,1,576]{1,3,2,0:T(8,128)(2,1)} %param.12) | copy-start | bytes 884740
  30.3 7.0 %copy-start.5 = (bf16[1,256,1,4]{1,3,2,0:T(4,128)(2,1)S(1)}, bf16[1,256,1,4]{1,3,2,0:T(4,128)(2,1)}, u32[]{:S(2)}) copy-start(bf16[1,256,1,4]{1,3,2,0:T(4,128)(2,1)} %param.13) | copy-start | bytes 6148
  30.3 75.4 %all-to-all-start.2 = ((bf16[16,32,3584]{2,1,0:T(8,128)(2,1)}), bf16[16,32,3584]{2,1,0:T(8,128)(2,1)}, u32[]{:S(2)}, u32[]{:S(2)}) async-start(bf16[16,32,3584]{2,1,0:T(8,128)(2,1)} %bitcast.117), calls=%async_computation.2 | async-start | bytes 7340032 | tf_op jit(solution)/shard_map/all_to_all | solution.py:163
  37.6 68.0 %collective-permute-start = (bf16[256,640]{1,0:T(8,128)(2,1)S(1)}, bf16[256,640]{1,0:T(8,128)(2,1)}, u32[]{:S(2)}, u32[]{:S(2)}) collective-permute-start(bf16[256,640]{1,0:T(8,128)(2,1)S(1)} %convolution_convert_fusion.3), channel_id=1, source_target_pairs={{0,128},{128,0},{1,129},{129,1},{2,130},{130,2},{3,131},{131,3},{4... | collective-permute-start | bytes 983048 | tf_op jit(solution)/shard_map/ppermute | solution.py:124
  105.7 20.2 %all-to-all-start = ((bf16[16,16,640]{2,1,0:T(8,128)(2,1)}), bf16[16,16,640]{2,1,0:T(8,128)(2,1)S(1)}, u32[]{:S(2)}, u32[]{:S(2)}) async-start(bf16[16,16,640]{2,1,0:T(8,128)(2,1)} %bitcast.3), calls=%async_computation | async-start | bytes 655360 | tf_op jit(solution)/shard_map/all_to_all | solution.py:125
  125.9 6.9 %copy-start = (bf16[1,2,4,64,576]{4,3,2,1,0:T(8,128)(2,1)S(1)}, bf16[1,2,4,64,576]{4,3,2,1,0:T(8,128)(2,1)}, u32[]{:S(2)}) copy-start(bf16[1,2,4,64,576]{4,3,2,1,0:T(8,128)(2,1)} %param.16) | copy-start | bytes 1769476
  125.9 6.9 %copy-start.1 = (bf16[1,2,4,576]{3,2,1,0:T(4,128)(2,1)S(1)}, bf16[1,2,4,576]{3,2,1,0:T(4,128)(2,1)}, u32[]{:S(2)}) copy-start(bf16[1,2,4,576]{3,2,1,0:T(4,128)(2,1)} %param.17) | copy-start | bytes 27652
  125.9 66.4 %all-to-all-start.3 = ((bf16[16,32,3584]{2,1,0:T(8,128)(2,1)}), bf16[16,32,3584]{2,1,0:T(8,128)(2,1)}, u32[]{:S(2)}, u32[]{:S(2)}) async-start(bf16[16,32,3584]{2,1,0:T(8,128)(2,1)} %bitcast.119), calls=%async_computation.3 | async-start | bytes 7340032 | tf_op jit(solution)/shard_map/all_to_all | solution.py:169
  192.3 14.8 %all-to-all-start.1 = ((bf16[8,32,640]{2,1,0:T(8,128)(2,1)}), bf16[8,32,640]{2,1,0:T(8,128)(2,1)S(1)}, u32[]{:S(2)}, u32[]{:S(2)}) async-start(bf16[8,32,640]{2,1,0:T(8,128)(2,1)} %bitcast.5), calls=%async_computation.1 | async-start | bytes 655360 | tf_op jit(solution)/shard_map/all_to_all | solution.py:132
  207.1 33.0 %all-to-all-start.4 = ((bf16[16,8,3584]{2,1,0:T(8,128)(2,1)}), bf16[16,8,3584]{2,1,0:T(8,128)(2,1)S(1)}, u32[]{:S(2)}, u32[]{:S(2)}) async-start(bf16[16,8,3584]{2,1,0:T(8,128)(2,1)} %fusion.1), calls=%async_computation.4 | async-start | bytes 1835008 | tf_op jit(solution)/shard_map/all_to_all | solution.py:180

commit v2 on v1

v2 whole, which is shorter than its diff:
```python
import jax
import jax.numpy as jnp
from jax import lax
from jax.experimental import pallas as pl
from jax.experimental.pallas import tpu as pltpu
from jax.sharding import Mesh, PartitionSpec as P

STEPS = 4
LAT = 512
ROPE = 64
QB = 128
D = 3584
TOP = 8
CAP = 2

Y, XH, Z, CORE = 4, 2, 8, 2
PLANE = Y * XH
LINE = Z * CORE
KEEP = LINE * CAP
ROW = 640
SIDE = 384

SCORE_SCALE = 192.0 ** (-0.5)
NEGATIVE = -1e30

LINE_AXES = ("z", "core")
PLANE_AXES = ("y", "xh")
CROSS_AXES = ("pool", "y", "xh")
EP_AXES = ("y", "xh", "z", "core")


WIDE = D + 128
BLOCK = 512
MIB = 1 << 20


def dispatch_kernel(own_ref, line_ref, kept_ref, given_ref, sent_ref, mix_ref):
    group, zc = own_ref[0], own_ref[1]
    tokens = line_ref.shape[0]
    routing = line_ref[:, D:].astype(jnp.float32).T
    token = lax.broadcasted_iota(jnp.int32, (tokens, tokens), 0)
    other = lax.broadcasted_iota(jnp.int32, (tokens, tokens), 1)
    ids = routing[:TOP].astype(jnp.int32)
    weights = routing[TOP : 2 * TOP] + routing[2 * TOP : 3 * TOP] + routing[3 * TOP : 4 * TOP]
    hits, shares = [], []
    for place in range(PLANE):
        named = ids == place * LINE + zc
        hits.append(jnp.sum(jnp.where(named, 1.0, 0.0), axis=0, keepdims=True))
        shares.append(jnp.sum(jnp.where(named, weights, 0.0), axis=0, keepdims=True))
    hit = jnp.concatenate(hits, axis=0)
    rank = jnp.dot(
        hit.astype(jnp.bfloat16),
        jnp.where(token < other, 1.0, 0.0).astype(jnp.bfloat16),
        preferred_element_type=jnp.float32,
    )
    rank = jnp.where(hit > 0.0, rank, -1.0).astype(jnp.int32)
    seat = lax.broadcasted_iota(jnp.int32, (KEEP, tokens), 0)
    chosen = [seat == rank[place : place + 1] for place in range(PLANE)]
    choose = jnp.concatenate([jnp.where(c, 1.0, 0.0) for c in chosen], axis=0)
    choose = choose.astype(jnp.bfloat16)
    group_of = Z * tokens // LINE
    device = tokens // LINE
    source = (other % group_of) // device * (CORE * device) + other // group_of * device
    source = source + other % device
    regroup = jnp.where(token == source, 1.0, 0.0).astype(jnp.bfloat16)
    mix = jnp.concatenate(
        [jnp.where(chosen[place], shares[place], 0.0) for place in range(PLANE)], axis=0
    )
    high = mix.astype(jnp.bfloat16)
    low = (mix - high.astype(jnp.float32)).astype(jnp.bfloat16)
    for index, part in enumerate((high, low)):
        turned_part = lax.dot_general(
            regroup, part, (((0,), (1,)), ((), ())), preferred_element_type=jnp.float32
        ).astype(jnp.bfloat16)
        mix_ref[index] = jnp.concatenate([turned_part, turned_part], axis=1)
    count = PLANE * KEEP
    for start in range(0, D, BLOCK):
        columns = pl.ds(start, BLOCK)
        rows = jnp.dot(choose, line_ref[:, columns], preferred_element_type=jnp.float32)
        rows = rows.astype(jnp.bfloat16)
        sent_ref[pl.ds(0, count), columns] = rows
        sent_ref[pl.ds(count, count), columns] = rows
    for half, ref in ((group, given_ref), (1 - group, kept_ref)):
        for place in range(PLANE):
            top = pl.multiple_of(half * count + place * KEEP, KEEP)
            rows = ref[pl.ds(place * LINE, LINE), :]
            sent_ref[pl.ds(top, LINE), pl.ds(D, SIDE)] = rows[:, :SIDE]
            tail = jnp.concatenate(
                [rows[:, SIDE:], jnp.zeros((LINE, 2 * SIDE - ROW), jnp.bfloat16)], axis=1
            )
            sent_ref[pl.ds(top + LINE, LINE), pl.ds(D, SIDE)] = tail


def dispatch(own, line, kept, given):
    tokens = line.shape[0]
    count = 2 * PLANE * KEEP
    vmem = pl.BlockSpec(memory_space=pltpu.VMEM)
    return pl.pallas_call(
        dispatch_kernel,
        out_shape=(
            jax.ShapeDtypeStruct((count, D + SIDE), jnp.bfloat16),
            jax.ShapeDtypeStruct((2, tokens, count), jnp.bfloat16),
        ),
        in_specs=[pl.BlockSpec(memory_space=pltpu.SMEM), vmem, vmem, vmem],
        out_specs=(vmem, vmem),
        compiler_params=pltpu.CompilerParams(vmem_limit_bytes=24 * MIB),
        name="dispatch",
    )(own, line, kept, given)


def turn_kernel(one_ref, two_ref, three_ref, out_ref):
    rows = out_ref.shape[0]
    slot_dev = out_ref.shape[1] // ROW
    to = lax.broadcasted_iota(jnp.int32, (rows, rows), 0)
    at = lax.broadcasted_iota(jnp.int32, (rows, rows), 1)
    core, z, yx = to // (Z * PLANE), to // PLANE % Z, to % PLANE
    turn = jnp.where(at == yx * LINE + z * CORE + core, 1.0, 0.0).astype(jnp.bfloat16)
    for b in range(slot_dev):
        heads, tails = [], []
        for place in range(b * PLANE, (b + 1) * PLANE):
            first = pl.ds(place * KEEP, LINE)
            second = pl.ds(place * KEEP + LINE, LINE)
            heads.append(
                jnp.concatenate([r[first, :] for r in (one_ref, two_ref, three_ref)], axis=1)
            )
            tails.append(jnp.concatenate([r[second, :] for r in (one_ref, two_ref)], axis=1))
        for parts, start in ((heads, 0), (tails, SIDE)):
            part = jnp.concatenate(parts, axis=0)
            moved = jnp.dot(turn, part, preferred_element_type=jnp.float32).astype(jnp.bfloat16)
            out_ref[:, pl.ds(b * ROW + start, part.shape[1])] = moved


def turned(taken, slot_dev):
    rows = taken.shape[0]
    shape = (PLANE * LINE, slot_dev * ROW)
    return pl.pallas_call(
        turn_kernel,
        grid=(1,),
        out_shape=jax.ShapeDtypeStruct(shape, jnp.bfloat16),
        in_specs=[
            pl.BlockSpec((rows, 128), lambda i, at=at: (0, D // 128 + at)) for at in range(3)
        ],
        out_specs=pl.BlockSpec(shape, lambda i: (0, 0)),
        compiler_params=pltpu.CompilerParams(vmem_limit_bytes=12 * MIB),
        name="turned",
    )(taken, taken, taken)


def expert_kernel(taken_ref, gate_ref, up_ref, down_ref, out_ref, inner, down, done):
    copy = pltpu.make_async_copy(down_ref, down, done)
    copy.start()
    width = inner.shape[1]
    for start in range(0, width, 256):
        columns = pl.ds(start, 256)
        rows = taken_ref[:, pl.ds(0, D)]
        gate = jnp.dot(rows, gate_ref[:, columns], preferred_element_type=jnp.float32)
        up = jnp.dot(rows, up_ref[:, columns], preferred_element_type=jnp.float32)
        inner[:, columns] = (jax.nn.silu(gate) * up).astype(jnp.bfloat16)
    copy.wait()
    for start in range(0, D, BLOCK):
        columns = pl.ds(start, BLOCK)
        out_ref[:, columns] = jnp.dot(
            inner[...], down[:, columns], preferred_element_type=jnp.float32
        ).astype(jnp.bfloat16)


def expert(taken, gate, up, down):
    count, width = taken.shape[0], gate.shape[1]
    vmem = pl.BlockSpec(memory_space=pltpu.VMEM)
    return pl.pallas_call(
        expert_kernel,
        out_shape=jax.ShapeDtypeStruct((count, D), jnp.bfloat16),
        in_specs=[vmem, vmem, vmem, pl.BlockSpec(memory_space=pl.ANY)],
        out_specs=vmem,
        scratch_shapes=[
            pltpu.VMEM((count, width), jnp.bfloat16),
            pltpu.VMEM((width, D), jnp.bfloat16),
            pltpu.SemaphoreType.DMA,
        ],
        compiler_params=pltpu.CompilerParams(vmem_limit_bytes=28 * MIB),
        cost_estimate=pl.CostEstimate(
            flops=6 * count * width * D, bytes_accessed=6 * width * D + 4 * count * D, transcendentals=0
        ),
        name="expert",
    )(taken, gate, up, down)


def combine_kernel(mix_ref, back_ref, beside_ref, out_ref):
    for start in range(0, D, BLOCK):
        columns = pl.ds(start, BLOCK)
        back = back_ref[:, columns]
        total = jnp.dot(mix_ref[0], back, preferred_element_type=jnp.float32)
        total = total + jnp.dot(mix_ref[1], back, preferred_element_type=jnp.float32)
        out_ref[:, columns] = total.astype(jnp.bfloat16)
    out_ref[:, pl.ds(D, beside_ref.shape[1])] = beside_ref[...]


def combine(mix, back, beside):
    vmem = pl.BlockSpec(memory_space=pltpu.VMEM)
    return pl.pallas_call(
        combine_kernel,
        out_shape=jax.ShapeDtypeStruct((mix.shape[1], D + beside.shape[1]), jnp.bfloat16),
        in_specs=[vmem, vmem, vmem],
        out_specs=vmem,
        compiler_params=pltpu.CompilerParams(vmem_limit_bytes=12 * MIB),
        name="combine",
    )(mix, back, beside)


def pair_kernel(pair_ref, out_ref):
    total = pair_ref[0, :, pl.ds(0, D)].astype(jnp.float32)
    for core in range(1, CORE):
        total = total + pair_ref[core, :, pl.ds(0, D)].astype(jnp.float32)
    out_ref[:, pl.ds(0, D)] = total.astype(jnp.bfloat16)
    beside = pair_ref.shape[2] - D
    for core in range(CORE):
        out_ref[:, pl.ds(D + core * beside, beside)] = pair_ref[core, :, pl.ds(D, beside)]


def paired(pair):
    cores, rows, width = pair.shape
    vmem = pl.BlockSpec(memory_space=pltpu.VMEM)
    return pl.pallas_call(
        pair_kernel,
        out_shape=jax.ShapeDtypeStruct((rows, D + cores * (width - D)), jnp.bfloat16),
        in_specs=[vmem],
        out_specs=vmem,
        compiler_params=pltpu.CompilerParams(vmem_limit_bytes=12 * MIB),
        name="paired",
    )(pair)


def prepare_kernel(
    own_ref, assign_ref, cache_ref, scale_ref, hidden_ref, ids_ref, weights_ref,
    kept_ref, given_ref, tokens_ref,
):
    group = own_ref[0]
    slot_dev = hidden_ref.shape[0]
    half_slots = kept_ref.shape[0]
    requests = assign_ref.shape[1]
    hidden = [hidden_ref[b].astype(jnp.float32) for b in range(slot_dev)]
    tokens_ref[:, pl.ds(0, D)] = jnp.concatenate(hidden, axis=0).astype(jnp.bfloat16)
    ids = jnp.concatenate([ids_ref[b].astype(jnp.float32) for b in range(slot_dev)], axis=0)
    rest = jnp.concatenate([weights_ref[b] for b in range(slot_dev)], axis=0)
    terms = [ids.astype(jnp.bfloat16)]
    for _ in range(3):
        term = rest.astype(jnp.bfloat16)
        rest = rest - term.astype(jnp.float32)
        terms.append(term)
    at = lax.broadcasted_iota(jnp.int32, (TOP, WIDE - D), 0)
    lane = lax.broadcasted_iota(jnp.int32, (TOP, WIDE - D), 1)
    routing = sum(
        jnp.dot(
            term,
            jnp.where(lane == at + TOP * index, 1.0, 0.0).astype(jnp.bfloat16),
            preferred_element_type=jnp.float32,
        )
        for index, term in enumerate(terms)
    )
    tokens_ref[:, pl.ds(D, WIDE - D)] = routing.astype(jnp.bfloat16)
    row = jnp.where(group == 0, assign_ref[0:1, :], assign_ref[1:2, :])
    tail = jnp.concatenate(
        [
            scale_ref[...].astype(jnp.float32),
            jnp.zeros((ROW - LAT - ROPE - LAT // QB, requests), jnp.float32),
        ],
        axis=0,
    ).astype(jnp.bfloat16)
    stored = jnp.concatenate([cache_ref[...], tail], axis=0)
    place = lax.broadcasted_iota(jnp.int32, (half_slots, requests), 0) * slot_dev
    for half, ref in ((group, kept_ref), (1 - group, given_ref)):
        choose = jnp.where(place + half == row, 1.0, 0.0).astype(jnp.bfloat16)
        ref[...] = lax.dot_general(
            choose, stored, (((1,), (1,)), ((), ())), preferred_element_type=jnp.float32
        ).astype(jnp.bfloat16)


def prepare(own, assign, cache, scale, hidden, ids, weights):
    half_slots = assign.shape[1] // hidden.shape[0]
    tokens = hidden.shape[0] * STEPS
    args = (own, assign, cache, scale, hidden, ids, weights)
    shapes = ((half_slots, ROW), (half_slots, ROW), (tokens, WIDE))

    def whole(shape):
        return pl.BlockSpec(shape, lambda i: (0,) * len(shape))

    return pl.pallas_call(
        prepare_kernel,
        grid=(1,),
        out_shape=[jax.ShapeDtypeStruct(shape, jnp.bfloat16) for shape in shapes],
        in_specs=[pl.BlockSpec(memory_space=pltpu.SMEM)] + [whole(a.shape) for a in args[1:]],
        out_specs=[whole(shape) for shape in shapes],
        compiler_params=pltpu.CompilerParams(vmem_limit_bytes=58 * MIB),
        name="prepare",
    )(*args)


def finish_kernel(
    own_ref, assign_ref, lengths_ref, gathered_ref, query_ref, fresh_ref, out_ref, moe_ref
):
    group, zc, yx = own_ref[0], own_ref[1], own_ref[2]
    slot_dev, rows = query_ref.shape[:2]
    lines, width = gathered_ref.shape
    positions = CORE * lines
    blocks = LAT // QB
    device = slot_dev * STEPS
    total = sum(
        gathered_ref[pl.ds(z * device, device), pl.ds(0, D)].astype(jnp.float32) for z in range(Z)
    ).astype(jnp.bfloat16)
    for b in range(slot_dev):
        moe_ref[b] = total[b * STEPS : (b + 1) * STEPS]
    assigned = jnp.where(group == 0, assign_ref[1:2, :], assign_ref[0:1, :])
    lengths = jnp.where(group == 0, lengths_ref[1:2, :], lengths_ref[0:1, :])
    lane = lax.broadcasted_iota(jnp.int32, (rows, positions), 1)
    position = lane % PLANE * LINE + lane // PLANE % Z * CORE + lane // lines
    new = 16
    step = lax.broadcasted_iota(jnp.int32, (rows, new), 0) // (rows // STEPS)
    token = lax.broadcasted_iota(jnp.int32, (rows, new), 1)
    by_rows = (((1,), (1,)), ((), ()))
    for b in range(slot_dev):
        slot = (yx * LINE + zc) * slot_dev + b
        length = jnp.sum(jnp.where(assigned == slot, lengths, 0), axis=1, keepdims=True)
        keys = jnp.concatenate(
            [
                gathered_ref[:, pl.ds(D + (core * slot_dev + b) * ROW, ROW)]
                for core in range(CORE)
            ],
            axis=0,
        )
        scale = keys[:, LAT:].astype(jnp.float32).T[ROPE : ROPE + blocks]
        score = lax.dot_general(
            query_ref[b, :, pl.ds(LAT, ROPE)],
            keys[:, LAT : LAT + ROPE],
            by_rows,
            preferred_element_type=jnp.float32,
        )
        for n in range(blocks):
            part = lax.dot_general(
                query_ref[b, :, pl.ds(n * QB, QB)],
                keys[:, n * QB : (n + 1) * QB],
                by_rows,
                preferred_element_type=jnp.float32,
            )
            score = score + part * scale[n : n + 1]
        score = jnp.where(position < length, score * SCORE_SCALE, NEGATIVE)
        fresh = jnp.concatenate(
            [fresh_ref[b].astype(jnp.float32), jnp.zeros((new - STEPS, LAT + ROPE), jnp.float32)],
            axis=0,
        ).astype(jnp.bfloat16)
        score_fresh = lax.dot_general(
            query_ref[b], fresh, by_rows, preferred_element_type=jnp.float32
        )
        score_fresh = jnp.where(token <= step, score_fresh * SCORE_SCALE, NEGATIVE)
        top = jnp.maximum(
            jnp.max(score, axis=1, keepdims=True), jnp.max(score_fresh, axis=1, keepdims=True)
        )
        exp_cache, exp_fresh = jnp.exp(score - top), jnp.exp(score_fresh - top)
        summed = jnp.sum(exp_cache, axis=1, keepdims=True)
        summed = summed + jnp.sum(exp_fresh, axis=1, keepdims=True)
        prob = exp_cache / summed
        weight_fresh = (exp_fresh / summed).astype(jnp.bfloat16)
        for n in range(blocks):
            columns = slice(n * QB, (n + 1) * QB)
            weight = (prob * scale[n : n + 1]).astype(jnp.bfloat16)
            latent = jnp.dot(weight, keys[:, columns], preferred_element_type=jnp.float32)
            latent = latent + jnp.dot(
                weight_fresh, fresh[:, columns], preferred_element_type=jnp.float32
            )
            out_ref[b, :, pl.ds(n * QB, QB)] = latent.astype(jnp.bfloat16)


def finish(own, assign, lengths, gathered, queries, fresh):
    slot_dev, rows = queries.shape[:2]
    vmem = pl.BlockSpec(memory_space=pltpu.VMEM)
    return pl.pallas_call(
        finish_kernel,
        out_shape=(
            jax.ShapeDtypeStruct((slot_dev, rows, LAT), jnp.bfloat16),
            jax.ShapeDtypeStruct((slot_dev, STEPS, D), jnp.bfloat16),
        ),
        in_specs=[pl.BlockSpec(memory_space=pltpu.SMEM)] + [vmem] * 5,
        out_specs=(vmem, vmem),
        compiler_params=pltpu.CompilerParams(vmem_limit_bytes=16 * MIB),
        name="finish",
    )(own, assign, lengths, gathered, queries, fresh)


def on_device(
    cache,
    cache_scale,
    lengths,
    assign,
    queries,
    new_kv,
    hidden,
    expert_ids,
    expert_weights,
    gate_w,
    up_w,
    down_w,
):
    slot_dev, heads = queries.shape[1], queries.shape[3]
    token_count = slot_dev * STEPS
    own = jnp.stack(
        [lax.axis_index("pool"), lax.axis_index(LINE_AXES), lax.axis_index(PLANE_AXES)]
    ).astype(jnp.int32)
    kept, given, token_rows = prepare(
        own,
        assign,
        cache[0, :, 0, :].T,
        cache_scale[0, :, 0, :].T,
        hidden[0],
        expert_ids[0],
        expert_weights[0],
    )
    given = lax.ppermute(given, "pool", [(0, 1), (1, 0)])
    line = lax.all_gather(token_rows, LINE_AXES, axis=0, tiled=True)
    line, given = lax.optimization_barrier((line, given))

    sent, mix = dispatch(own, line, kept, given)
    taken = lax.all_to_all(
        sent.reshape(2 * PLANE, KEEP, D + SIDE), CROSS_AXES, 0, 0, tiled=True
    ).reshape(2 * PLANE * KEEP, D + SIDE)

    served = expert(taken, gate_w[0], up_w[0], down_w[0])

    beside = turned(taken, slot_dev)
    served, beside = lax.optimization_barrier((served, beside))
    back = lax.all_to_all(
        served.reshape(2 * PLANE, KEEP, D), CROSS_AXES, 0, 0, tiled=True
    ).reshape(2 * PLANE * KEEP, D)

    mixed = combine(mix, back, beside).reshape(CORE, Z * token_count, -1)
    pair = paired(lax.all_to_all(mixed, "core", 0, 0, tiled=True))
    gathered = lax.all_to_all(pair.reshape(Z, token_count, -1), "z", 0, 0, tiled=True)
    context, moe_out = finish(
        own,
        assign,
        lengths,
        gathered.reshape(pair.shape),
        queries[0].reshape(slot_dev, STEPS * heads, -1),
        new_kv[0],
    )
    return (
        context.reshape(1, slot_dev, STEPS, heads, LAT),
        moe_out.reshape(1, slot_dev, STEPS, D),
    )


def solution(mesh):
    fine = Mesh(
        mesh.devices.reshape(2, Y, XH, Z, CORE), ("pool", "y", "xh", "z", "core")
    )
    return jax.shard_map(
        on_device,
        mesh=fine,
        in_specs=(
            P("pool", None, EP_AXES, None),
            P("pool", None, EP_AXES, None),
            P(),
            P(),
            P("pool", EP_AXES, None, None, None),
            P("pool", EP_AXES, None, None),
            P("pool", EP_AXES, None, None),
            P("pool", EP_AXES, None, None),
            P("pool", EP_AXES, None, None),
            P(EP_AXES, None, "pool"),
            P(EP_AXES, None, "pool"),
            P(EP_AXES, "pool", None),
        ),
        out_specs=(P("pool", EP_AXES, None, None, None), P("pool", EP_AXES, None, None)),
        check_vma=False,
    )
```

time: 242 us -> 182 us (0.75)
  waiting for transfers between devices: 148 us -> 0.01 us
  blocking collectives: 23.9 us -> 157 us
  starting transfers between devices: 33.9 us -> 2.04 us
  matrix products: 26.3 us -> 0 us
  Pallas kernels: 0 us -> 14.2 us
  other arithmetic: 5.1 us -> 0.65 us
  local copies, waits for them, and re-layouts: 2.49 us -> 5.54 us
    all_to_all x0 -> x4, blocking collectives: none -> 134 us  [the longest x1 54.7 us: on_device(): lax.all_to_all(sent.reshape(2 * PLANE, KEEP, D + SIDE), CROSS_AXES, 0, 0,...]
    all_to_all x5 -> x0, waiting for transfers between devices: 81.5 us -> none  [the longest x1 58 us: on_device(): lax.all_to_all(served.reshape(2 * PLANE, KEEP, D), CROSS_AXES, 0, 0, tile...]
    ppermute x1, waiting for transfers between devices: 66.6 us -> 0.01 us  [on_device(): given = lax.ppermute(given, 'pool', [(0, 1), (1, 0)])]
    all_to_all x5 -> x0, starting transfers between devices: 32.5 us -> none  [the longest x1 7.65 us: on_device(): lax.all_to_all(mixed.reshape(LINE, token_count, D), LINE_AXES, 0, 0, tile...]
    dot_general x12 -> x0, matrix products: 26 us -> none  [the longest x1 10.1 us: on_device(): jnp.dot(inner, down_w[0], preferred_element_type=jnp.float32)]
    pallas_call x0 -> x7, Pallas kernels: none -> 14.2 us  [the longest x1 6.36 us: expert(): pl.pallas_call(expert_kernel, out_shape=jax.ShapeDtypeStruct((count, D),...]
    unnamed x17 -> x20, local copies, waits for them, and re-layouts: 0.39 us -> 5.54 us
  transfers between devices with their start and end apart: 6 -> 1, of which waited for: 4 -> 0; matrix products, arithmetic and copies ran while one was open for 11% -> 0% of each run, Pallas kernels for 0% -> 0%
where the time goes in v2:
time: 182 us; the launch traced here: 181 us
  blocking collectives  157 us (86%)
  Pallas kernels  14.2 us (8%)
  local copies, waits for them, and re-layouts  5.54 us (3%)
  starting transfers between devices  2.04 us (1%)
    all_to_all x1, blocking collectives, on_device(): lax.all_to_all(sent.reshape(2 * PLANE, KEEP, D + SIDE), CROSS_AXES, 0, 0,...  54.7 us
    all_to_all x1, blocking collectives, on_device(): lax.all_to_all(served.reshape(2 * PLANE, KEEP, D), CROSS_AXES, 0, 0, tile...  46.2 us
    all_to_all x1, blocking collectives, on_device(): lax.all_to_all(pair.reshape(Z, token_count, -1), 'z', 0, 0, tiled=True)  25 us
    all_gather x1, blocking collectives, on_device(): line = lax.all_gather(token_rows, LINE_AXES, axis=0, tiled=True)  23.6 us
    all_to_all x1, blocking collectives, on_device(): pair = paired(lax.all_to_all(mixed, 'core', 0, 0, tiled=True))  7.9 us
    pallas_call x1, Pallas kernels, expert(): pl.pallas_call(expert_kernel, out_shape=jax.ShapeDtypeStruct((count, D),...  6.36 us
    unnamed x20, local copies, waits for them, and re-layouts  5.54 us
  transfers between devices with their start and end apart: 1, of which 0 were waited for; matrix products, arithmetic and copies ran while one was open for 0% of the time, Pallas kernels for 0%

profile of v2, /device:TPU:1, one launch (start us, length us, event | category | flops | bytes accessed | tf_op | source)
XLA Modules:
  0.0 180.6 jit_solution(7348497609201436319)
XLA Ops:
  0.6 0.7 pad_add_fusion.own_ref
  1.3 2.0 %prepare.1 = (bf16[128,640]{1,0:T(8,128)(2,1)}, bf16[128,640]{1,0:T(8,128)(2,1)}, bf16[8,3712]{1,0:T(8,128)(2,1)}) custom-call(s32[3]{0:T(128)} %pad_add_fusion.own_ref, s32[2,256]{1,0:T(2,128)} %assign_ref.3, bf16[576,256]{1,0:T(8,128)(2,1)} %bitcast.41, bf16[4,256]{1,0:T(4,128)(2,1)} %bitcast.45, bf16[2,4,3584]{2,1,0:T(4,128)(2,1)} %bitcast.42, ...), custom_call_target="tpu_custom_call" | custom-call | tf_op jit(solution)/shard_map/prepare/pallas_call | solution.py:287
  3.3 2.0 %collective-permute-start = (bf16[128,640]{1,0:T(8,128)(2,1)}, bf16[128,640]{1,0:T(8,128)(2,1)S(1)}, u32[]{:S(2)}, u32[]{:S(2)}) collective-permute-start(bf16[128,640]{1,0:T(8,128)(2,1)} %get-tuple-element.14), channel_id=1, source_target_pairs={{0,128},{128,0},{1,129},{129,1},{2,130},{130,2},{3,131},{131,3},{4... | collective-permute-start | bytes 491528 | tf_op jit(solution)/shard_map/ppermute | solution.py:416
  5.3 23.6 %all_gather.3.line_ref = bf16[128,3712]{1,0:T(8,128)(2,1)S(1)} all-gather(bf16[8,3712]{1,0:T(8,128)(2,1)} %get-tuple-element.13), channel_id=1, replica_groups=mesh['pool'=2,'y'=4,'xh'=2,'z'=8,'core'=2] {'z','core'}, dimensions={0}, use_global_device_ids=true | all-gather | bytes 1009664 | tf_op jit(solution)/shard_map/all_gather | solution.py:417
  28.9 0.0 collective-permute-done.given_ref
  28.9 0.9 copy-done.1
  29.9 0.7 copy-done.4
  30.5 1.5 dispatch.1
  32.0 54.7 %all_to_all.20 = bf16[16,32,3968]{2,1,0:T(8,128)(2,1)S(1)} all-to-all(bf16[16,32,3968]{2,1,0:T(8,128)(2,1)S(1)} %bitcast.32), channel_id=1, replica_groups=mesh['pool'=2,'y'=4,'xh'=2,'z'=8,'core'=2] {'pool','y','xh'}, dimensions={0} | all-to-all | bytes 8126464 | tf_op jit(solution)/shard_map/all_to_all | solution.py:421
  86.7 0.3 turned.1.beside_ref
  87.0 1.8 copy-done.7
  88.8 1.1 copy-done.8
  89.9 1.0 copy-done.9
  90.9 6.4 %expert.1 = bf16[512,3584]{1,0:T(8,128)(2,1)S(1)} custom-call(bf16[512,3968]{1,0:T(8,128)(2,1)S(1)} %bitcast.29, bf16[3584,512]{1,0:T(8,128)(2,1)S(1)} %bitcast.38, bf16[3584,512]{1,0:T(8,128)(2,1)S(1)} %bitcast.39, bf16[512,3584]{1,0:T(8,128)(2,1)S(1)} %bitcast.40), custom_call_target="tpu_custom_call" | custom-call | flops 5637144576 | bytes 18350080 | tf_op jit(solution)/shard_map/expert/pallas_call | solution.py:170
  97.3 46.2 %all_to_all.21 = bf16[16,32,3584]{2,1,0:T(8,128)(2,1)S(1)} all-to-all(bf16[16,32,3584]{2,1,0:T(8,128)(2,1)S(1)} %bitcast.33), channel_id=1, replica_groups=mesh['pool'=2,'y'=4,'xh'=2,'z'=8,'core'=2] {'pool','y','xh'}, dimensions={0} | all-to-all | bytes 7340032 | tf_op jit(solution)/shard_map/all_to_all | solution.py:429
  143.5 1.2 combine.1
  144.6 0.0 copy-start
  144.6 0.0 copy-start.2
  144.7 0.0 copy-start.3
  144.7 0.0 copy-start.6
  144.7 7.9 %all_to_all.22.pair_ref = bf16[2,64,4864]{2,1,0:T(8,128)(2,1)S(1)} all-to-all(bf16[2,64,4864]{2,1,0:T(8,128)(2,1)S(1)} %bitcast.31), channel_id=1, replica_groups=mesh['pool'=2,'y'=4,'xh'=2,'z'=8,'core'=2] {'core'}, dimensions={0} | all-to-all | bytes 2490368 | tf_op jit(solution)/shard_map/all_to_all | solution.py:434
  152.6 0.1 paired.1
  152.7 25.0 %all_to_all.23 = bf16[8,8,6144]{2,1,0:T(8,128)(2,1)S(1)} all-to-all(bf16[8,8,6144]{2,1,0:T(8,128)(2,1)S(1)} %bitcast.35), channel_id=1, replica_groups=mesh['pool'=2,'y'=4,'xh'=2,'z'=8,'core'=2] {'z'}, dimensions={0} | all-to-all | bytes 1572864 | tf_op jit(solution)/shard_map/all_to_all | solution.py:435
  177.7 2.9 %finish.1 = (bf16[2,256,512]{2,1,0:T(8,128)(2,1)}, bf16[2,4,3584]{2,1,0:T(4,128)(2,1)}) custom-call(s32[3]{0:T(128)S(1)} %copy-done.5, s32[2,256]{1,0:T(2,128)S(1)} %copy-done.3, s32[2,256]{1,0:T(2,128)S(1)} %copy-done.6, bf16[64,6144]{1,0:T(8,128)(2,1)S(1)} %bitcast.34, bf16[2,256,576]{2,1,0:T(8,128)(2,1)S(1)} %bitcast.36, bf16[2,4,576]{2,1,0:T(4,128)(2,1)S(1)} %bitcast.37), custom_call_target="tpu_custom_call" | custom-call | tf_op jit(solution)/shard_map/finish/pallas_call | solution.py:375
  (11 shorter events, 0.0 us)
Async XLA Ops:
  3.3 25.6 %collective-permute-start = (bf16[128,640]{1,0:T(8,128)(2,1)}, bf16[128,640]{1,0:T(8,128)(2,1)S(1)}, u32[]{:S(2)}, u32[]{:S(2)}) collective-permute-start(bf16[128,640]{1,0:T(8,128)(2,1)} %get-tuple-element.14), channel_id=1, source_target_pairs={{0,128},{128,0},{1,129},{129,1},{2,130},{130,2},{3,131},{131,3},{4... | collective-permute-start | bytes 491528 | tf_op jit(solution)/shard_map/ppermute | solution.py:416
  28.9 0.9 copy-start.1
  29.9 0.7 copy-start.4
  86.7 2.0 %copy-start.7 = (bf16[1,3584,512]{2,1,0:T(8,128)(2,1)S(1)}, bf16[1,3584,512]{2,1,0:T(8,128)(2,1)}, u32[]{:S(2)}) copy-start(bf16[1,3584,512]{2,1,0:T(8,128)(2,1)} %param.21) | copy-start | bytes 11010052
  86.7 3.2 %copy-start.8 = (bf16[1,3584,512]{2,1,0:T(8,128)(2,1)S(1)}, bf16[1,3584,512]{2,1,0:T(8,128)(2,1)}, u32[]{:S(2)}) copy-start(bf16[1,3584,512]{2,1,0:T(8,128)(2,1)} %param.22) | copy-start | bytes 11010052
  86.7 4.2 %copy-start.9 = (bf16[1,512,3584]{2,1,0:T(8,128)(2,1)S(1)}, bf16[1,512,3584]{2,1,0:T(8,128)(2,1)}, u32[]{:S(2)}) copy-start(bf16[1,512,3584]{2,1,0:T(8,128)(2,1)} %param.23) | copy-start | bytes 11010052
  144.6 33.1 %copy-start = (bf16[1,2,4,64,576]{4,3,2,1,0:T(8,128)(2,1)S(1)}, bf16[1,2,4,64,576]{4,3,2,1,0:T(8,128)(2,1)}, u32[]{:S(2)}) copy-start(bf16[1,2,4,64,576]{4,3,2,1,0:T(8,128)(2,1)} %param.16) | copy-start | bytes 1769476
  144.6 33.0 %copy-start.2 = (bf16[1,2,4,576]{3,2,1,0:T(4,128)(2,1)S(1)}, bf16[1,2,4,576]{3,2,1,0:T(4,128)(2,1)}, u32[]{:S(2)}) copy-start(bf16[1,2,4,576]{3,2,1,0:T(4,128)(2,1)} %param.17) | copy-start | bytes 27652
  144.7 33.0 %copy-start.3 = (s32[2,256]{1,0:T(2,128)S(1)}, s32[2,256]{1,0:T(2,128)}, u32[]{:S(2)}) copy-start(s32[2,256]{1,0:T(2,128)} %assign_ref.3) | copy-start | bytes 6148
  144.7 33.0 %copy-start.5 = (s32[3]{0:T(128)S(1)}, s32[3]{0:T(128)}, u32[]{:S(2)}) copy-start(s32[3]{0:T(128)} %pad_add_fusion.own_ref) | copy-start | bytes 40
  144.7 33.0 %copy-start.6 = (s32[2,256]{1,0:T(2,128)S(1)}, s32[2,256]{1,0:T(2,128)}, u32[]{:S(2)}) copy-start(s32[2,256]{1,0:T(2,128)} %lengths_ref.1) | copy-start | bytes 6148

commit v3 on v2

v3 whole, which is shorter than its diff:
```python
import jax
import jax.numpy as jnp
from jax import lax
from jax.experimental import pallas as pl
from jax.experimental.pallas import tpu as pltpu
from jax.sharding import Mesh, PartitionSpec as P

STEPS = 4
LAT = 512
ROPE = 64
QB = 128
D = 3584
TOP = 8
CAP = 2

Y, XH, LINE, ZL, CORE = 4, 2, 4, 2, 2
FOUR = ZL * CORE
PLANE = Y * XH * FOUR
KEEP = LINE * CAP
ROW = 640
SIDE = 384
SPREAD = 8

SCORE_SCALE = 192.0 ** (-0.5)
NEGATIVE = -1e30

LINE_AXES = "zh"
CROSS_AXES = ("pool", "y", "xh", "zl", "core")
EP_AXES = ("y", "xh", "zh", "zl", "core")


WIDE = D + 128
BLOCK = 512
MIB = 1 << 20


def whole(shape):
    return pl.BlockSpec(shape, lambda i: (0,) * len(shape))


def dispatch_kernel(line_ref, kept_ref, given_ref, sent_ref, mix_ref):
    group, zh = lax.axis_index("pool"), lax.axis_index(LINE_AXES)
    tokens = line_ref.shape[0]
    routing = jnp.concatenate(
        [line_ref[:, pl.ds(D, 128)].astype(jnp.float32), jnp.zeros((128 - tokens, 128), jnp.float32)],
        axis=0,
    ).T[:, :tokens]
    place = lax.broadcasted_iota(jnp.int32, (PLANE, tokens), 0)
    expert_at = place // FOUR * (LINE * FOUR) + zh * FOUR + place % FOUR
    hit = jnp.zeros((PLANE, tokens), jnp.float32)
    share = jnp.zeros((PLANE, tokens), jnp.float32)
    for k in range(TOP):
        weight = sum(routing[TOP * part + k : TOP * part + k + 1] for part in (1, 2, 3))
        named = routing[k : k + 1].astype(jnp.int32) == expert_at
        hit = hit + jnp.where(named, 1.0, 0.0)
        share = share + jnp.where(named, weight, 0.0)
    token = lax.broadcasted_iota(jnp.int32, (tokens, tokens), 0)
    other = lax.broadcasted_iota(jnp.int32, (tokens, tokens), 1)
    rank = jnp.dot(
        hit.astype(jnp.bfloat16),
        jnp.where(token < other, 1.0, 0.0).astype(jnp.bfloat16),
        preferred_element_type=jnp.float32,
    )
    rank = jnp.where(hit > 0.0, rank, -1.0).astype(jnp.int32)
    seat = lax.broadcasted_iota(jnp.int32, (KEEP, tokens), 0)
    chosen = [seat == rank[e : e + 1] for e in range(PLANE)]
    choose = jnp.concatenate([jnp.where(c, 1.0, 0.0) for c in chosen], axis=0)
    choose = choose.astype(jnp.bfloat16)
    mix = jnp.concatenate(
        [jnp.where(chosen[e], share[e : e + 1], 0.0) for e in range(PLANE)], axis=0
    )
    high = mix.astype(jnp.bfloat16)
    low = (mix - high.astype(jnp.float32)).astype(jnp.bfloat16)
    same = jnp.where(token == other, 1.0, 0.0).astype(jnp.bfloat16)
    for index, part in enumerate((high, low)):
        across = lax.dot_general(
            same, part, (((1,), (1,)), ((), ())), preferred_element_type=jnp.float32
        ).astype(jnp.bfloat16)
        mix_ref[index] = jnp.concatenate([across, across], axis=1)
    count = PLANE * KEEP
    for start in range(0, D, BLOCK):
        columns = pl.ds(start, BLOCK)
        rows = jnp.dot(choose, line_ref[:, columns], preferred_element_type=jnp.float32)
        rows = rows.astype(jnp.bfloat16)
        sent_ref[pl.ds(0, count), columns] = rows
        sent_ref[pl.ds(count, count), columns] = rows
    for half, ref in ((group, given_ref), (1 - group, kept_ref)):
        top = pl.multiple_of(half * count, count)
        sent_ref[pl.ds(top, count), pl.ds(D, SIDE)] = ref[...]


def dispatch(line, kept, given):
    tokens = line.shape[0]
    count = 2 * PLANE * KEEP
    vmem = pl.BlockSpec(memory_space=pltpu.VMEM)
    return pl.pallas_call(
        dispatch_kernel,
        out_shape=(
            jax.ShapeDtypeStruct((count, D + SIDE), jnp.bfloat16),
            jax.ShapeDtypeStruct((2, tokens, count), jnp.bfloat16),
        ),
        in_specs=[vmem, vmem, vmem],
        out_specs=(vmem, vmem),
        compiler_params=pltpu.CompilerParams(vmem_limit_bytes=24 * MIB),
        cost_estimate=pl.CostEstimate(
            flops=2 * count * tokens * D, bytes_accessed=8 * count * D, transcendentals=0
        ),
        name="dispatch",
    )(line, kept, given)


def turn_kernel(one_ref, two_ref, three_ref, out_ref):
    rows = out_ref.shape[0]
    group = SPREAD * KEEP
    to = lax.broadcasted_iota(jnp.int32, (rows, group), 0)
    at = lax.broadcasted_iota(jnp.int32, (rows, group), 1)
    first = to % SPREAD * KEEP + to // SPREAD
    for index in range(out_ref.shape[1] // ROW):
        block = pl.ds(index * group, group)
        three = jnp.concatenate([r[block, :] for r in (one_ref, two_ref, three_ref)], axis=1)
        for part, (start, width) in enumerate(((0, SIDE), (SIDE, ROW - SIDE))):
            turn = jnp.where(at == first + part * LINE, 1.0, 0.0).astype(jnp.bfloat16)
            moved = jnp.dot(turn, three[:, :width], preferred_element_type=jnp.float32)
            out_ref[:, pl.ds(index * ROW + start, width)] = moved.astype(jnp.bfloat16)


def turned(taken):
    rows = taken.shape[0]
    shape = (LINE * SPREAD, rows // (SPREAD * KEEP) * ROW)
    return pl.pallas_call(
        turn_kernel,
        grid=(1,),
        out_shape=jax.ShapeDtypeStruct(shape, jnp.bfloat16),
        in_specs=[
            pl.BlockSpec((rows, 128), lambda i, at=at: (0, D // 128 + at)) for at in range(3)
        ],
        out_specs=whole(shape),
        compiler_params=pltpu.CompilerParams(vmem_limit_bytes=12 * MIB),
        name="turned",
    )(taken, taken, taken)


def expert_kernel(taken_ref, gate_ref, up_ref, down_ref, out_ref, inner, down, done):
    copy = pltpu.make_async_copy(down_ref, down, done)
    copy.start()
    width = inner.shape[1]
    for start in range(0, width, 256):
        columns = pl.ds(start, 256)
        rows = taken_ref[:, pl.ds(0, D)]
        gate = jnp.dot(rows, gate_ref[:, columns], preferred_element_type=jnp.float32)
        up = jnp.dot(rows, up_ref[:, columns], preferred_element_type=jnp.float32)
        inner[:, columns] = (jax.nn.silu(gate) * up).astype(jnp.bfloat16)
    copy.wait()
    for start in range(0, D, BLOCK):
        columns = pl.ds(start, BLOCK)
        out_ref[:, columns] = jnp.dot(
            inner[...], down[:, columns], preferred_element_type=jnp.float32
        ).astype(jnp.bfloat16)


def expert(taken, gate, up, down):
    count, width = taken.shape[0], gate.shape[1]
    vmem = pl.BlockSpec(memory_space=pltpu.VMEM)
    return pl.pallas_call(
        expert_kernel,
        out_shape=jax.ShapeDtypeStruct((count, D), jnp.bfloat16),
        in_specs=[vmem, vmem, vmem, pl.BlockSpec(memory_space=pl.ANY)],
        out_specs=vmem,
        scratch_shapes=[
            pltpu.VMEM((count, width), jnp.bfloat16),
            pltpu.VMEM((width, D), jnp.bfloat16),
            pltpu.SemaphoreType.DMA,
        ],
        compiler_params=pltpu.CompilerParams(vmem_limit_bytes=28 * MIB),
        cost_estimate=pl.CostEstimate(
            flops=6 * count * width * D, bytes_accessed=6 * width * D + 4 * count * D, transcendentals=0
        ),
        name="expert",
    )(taken, gate, up, down)


def combine_kernel(mix_ref, back_ref, beside_ref, out_ref):
    for start in range(0, D, BLOCK):
        columns = pl.ds(start, BLOCK)
        back = back_ref[:, columns]
        total = jnp.dot(mix_ref[0], back, preferred_element_type=jnp.float32)
        total = total + jnp.dot(mix_ref[1], back, preferred_element_type=jnp.float32)
        out_ref[:, columns] = total.astype(jnp.bfloat16)
    out_ref[:, pl.ds(D, beside_ref.shape[1])] = beside_ref[...]


def combine(mix, back, beside):
    vmem = pl.BlockSpec(memory_space=pltpu.VMEM)
    return pl.pallas_call(
        combine_kernel,
        out_shape=jax.ShapeDtypeStruct((mix.shape[1], D + beside.shape[1]), jnp.bfloat16),
        in_specs=[vmem, vmem, vmem],
        out_specs=vmem,
        compiler_params=pltpu.CompilerParams(vmem_limit_bytes=12 * MIB),
        name="combine",
    )(mix, back, beside)


def prepare_kernel(
    assign_ref, cache_ref, scale_ref, hidden_ref, ids_ref, weights_ref,
    kept_ref, given_ref, tokens_ref,
):
    group = lax.axis_index("pool")
    slot_dev = hidden_ref.shape[0]
    requests = assign_ref.shape[1]
    hidden = [hidden_ref[b].astype(jnp.float32) for b in range(slot_dev)]
    hidden = jnp.concatenate(hidden, axis=0)
    ids = jnp.concatenate([ids_ref[b].astype(jnp.float32) for b in range(slot_dev)], axis=0)
    rest = jnp.concatenate([weights_ref[b] for b in range(slot_dev)], axis=0)
    terms = [ids.astype(jnp.bfloat16)]
    for _ in range(3):
        term = rest.astype(jnp.bfloat16)
        rest = rest - term.astype(jnp.float32)
        terms.append(term)
    at = lax.broadcasted_iota(jnp.int32, (TOP, WIDE - D), 0)
    lane = lax.broadcasted_iota(jnp.int32, (TOP, WIDE - D), 1)
    routing = sum(
        jnp.dot(
            term,
            jnp.where(lane == at + TOP * index, 1.0, 0.0).astype(jnp.bfloat16),
            preferred_element_type=jnp.float32,
        )
        for index, term in enumerate(terms)
    )
    row = jnp.concatenate([hidden, routing], axis=1)
    tokens_ref[...] = jnp.concatenate([row] * LINE, axis=0).astype(jnp.bfloat16)
    row = jnp.where(group == 0, assign_ref[0:1, :], assign_ref[1:2, :])
    tail = jnp.concatenate(
        [
            scale_ref[...].astype(jnp.float32),
            jnp.zeros((ROW - LAT - ROPE - LAT // QB, requests), jnp.float32),
        ],
        axis=0,
    ).astype(jnp.bfloat16)
    stored = jnp.concatenate([cache_ref[...], tail], axis=0)
    at = lax.broadcasted_iota(jnp.int32, (PLANE * KEEP, requests), 0)
    place, zh = at // KEEP, at % LINE
    slot = (place // FOUR * (LINE * FOUR) + zh * FOUR + place % FOUR) * slot_dev
    head = lax.broadcasted_iota(jnp.int32, (PLANE * KEEP, SIDE), 0) % KEEP < LINE
    for half, ref in ((group, kept_ref), (1 - group, given_ref)):
        choose = jnp.where(slot + half == row, 1.0, 0.0).astype(jnp.bfloat16)
        found = lax.dot_general(
            choose, stored, (((1,), (1,)), ((), ())), preferred_element_type=jnp.float32
        )
        tail = jnp.concatenate(
            [found[:, SIDE:], jnp.zeros((PLANE * KEEP, 2 * SIDE - ROW), jnp.float32)], axis=1
        )
        ref[...] = jnp.where(head, found[:, :SIDE], tail).astype(jnp.bfloat16)


def prepare(assign, cache, scale, hidden, ids, weights):
    tokens = LINE * hidden.shape[0] * STEPS
    args = (assign, cache, scale, hidden, ids, weights)
    shapes = ((PLANE * KEEP, SIDE), (PLANE * KEEP, SIDE), (tokens, WIDE))
    return pl.pallas_call(
        prepare_kernel,
        grid=(1,),
        out_shape=[jax.ShapeDtypeStruct(shape, jnp.bfloat16) for shape in shapes],
        in_specs=[whole(a.shape) for a in args],
        out_specs=[whole(shape) for shape in shapes],
        compiler_params=pltpu.CompilerParams(vmem_limit_bytes=58 * MIB),
        name="prepare",
    )(*args)


def finish_kernel(
    assign_ref, lengths_ref, gathered_ref, query_ref, fresh_ref, out_ref, moe_ref
):
    group, ep_index = lax.axis_index("pool"), lax.axis_index(EP_AXES)
    slot_dev, rows = query_ref.shape[:2]
    lines = gathered_ref.shape[0]
    parts = PLANE // SPREAD
    positions = parts * lines
    blocks = LAT // QB
    device = slot_dev * STEPS
    total = sum(
        gathered_ref[pl.ds(z * device, device), pl.ds(0, D)].astype(jnp.float32) for z in range(LINE)
    ).astype(jnp.bfloat16)
    for b in range(slot_dev):
        moe_ref[b] = total[b * STEPS : (b + 1) * STEPS]
    assigned = jnp.where(group == 0, assign_ref[1:2, :], assign_ref[0:1, :])
    lengths = jnp.where(group == 0, lengths_ref[1:2, :], lengths_ref[0:1, :])
    lane = lax.broadcasted_iota(jnp.int32, (rows, positions), 1)
    place = lane // lines * SPREAD + lane % SPREAD
    position = place // FOUR * (LINE * FOUR) + lane % lines // SPREAD * FOUR + place % FOUR
    new = 16
    step = lax.broadcasted_iota(jnp.int32, (rows, new), 0) // (rows // STEPS)
    token = lax.broadcasted_iota(jnp.int32, (rows, new), 1)
    by_rows = (((1,), (1,)), ((), ()))
    for b in range(slot_dev):
        slot = ep_index * slot_dev + b
        length = jnp.sum(jnp.where(assigned == slot, lengths, 0), axis=1, keepdims=True)
        keys = jnp.concatenate(
            [
                gathered_ref[:, pl.ds(D + (b * parts + part) * ROW, ROW)]
                for part in range(parts)
            ],
            axis=0,
        )
        scale = keys[:, LAT:].astype(jnp.float32).T[ROPE : ROPE + blocks]
        score = lax.dot_general(
            query_ref[b, :, pl.ds(LAT, ROPE)],
            keys[:, LAT : LAT + ROPE],
            by_rows,
            preferred_element_type=jnp.float32,
        )
        for n in range(blocks):
            part = lax.dot_general(
                query_ref[b, :, pl.ds(n * QB, QB)],
                keys[:, n * QB : (n + 1) * QB],
                by_rows,
                preferred_element_type=jnp.float32,
            )
            score = score + part * scale[n : n + 1]
        score = jnp.where(position < length, score * SCORE_SCALE, NEGATIVE)
        fresh = jnp.concatenate(
            [fresh_ref[b].astype(jnp.float32), jnp.zeros((new - STEPS, LAT + ROPE), jnp.float32)],
            axis=0,
        ).astype(jnp.bfloat16)
        score_fresh = lax.dot_general(
            query_ref[b], fresh, by_rows, preferred_element_type=jnp.float32
        )
        score_fresh = jnp.where(token <= step, score_fresh * SCORE_SCALE, NEGATIVE)
        top = jnp.maximum(
            jnp.max(score, axis=1, keepdims=True), jnp.max(score_fresh, axis=1, keepdims=True)
        )
        exp_cache, exp_fresh = jnp.exp(score - top), jnp.exp(score_fresh - top)
        summed = jnp.sum(exp_cache, axis=1, keepdims=True)
        summed = summed + jnp.sum(exp_fresh, axis=1, keepdims=True)
        prob = exp_cache / summed
        weight_fresh = (exp_fresh / summed).astype(jnp.bfloat16)
        for n in range(blocks):
            columns = slice(n * QB, (n + 1) * QB)
            weight = (prob * scale[n : n + 1]).astype(jnp.bfloat16)
            latent = jnp.dot(weight, keys[:, columns], preferred_element_type=jnp.float32)
            latent = latent + jnp.dot(
                weight_fresh, fresh[:, columns], preferred_element_type=jnp.float32
            )
            out_ref[b, :, pl.ds(n * QB, QB)] = latent.astype(jnp.bfloat16)


def finish(assign, lengths, gathered, queries, fresh):
    slot_dev, rows = queries.shape[:2]
    vmem = pl.BlockSpec(memory_space=pltpu.VMEM)
    return pl.pallas_call(
        finish_kernel,
        out_shape=(
            jax.ShapeDtypeStruct((slot_dev, rows, LAT), jnp.bfloat16),
            jax.ShapeDtypeStruct((slot_dev, STEPS, D), jnp.bfloat16),
        ),
        in_specs=[vmem] * 5,
        out_specs=(vmem, vmem),
        compiler_params=pltpu.CompilerParams(vmem_limit_bytes=16 * MIB),
        name="finish",
    )(assign, lengths, gathered, queries, fresh)


def on_device(
    cache,
    cache_scale,
    lengths,
    assign,
    queries,
    new_kv,
    hidden,
    expert_ids,
    expert_weights,
    gate_w,
    up_w,
    down_w,
):
    slot_dev, heads = queries.shape[1], queries.shape[3]
    token_count = slot_dev * STEPS
    kept, given, token_rows = prepare(
        assign,
        cache[0, :, 0, :].T,
        cache_scale[0, :, 0, :].T,
        hidden[0],
        expert_ids[0],
        expert_weights[0],
    )
    given = lax.ppermute(given, "pool", [(0, 1), (1, 0)])
    line = lax.all_to_all(
        token_rows.reshape(LINE, token_count, WIDE), LINE_AXES, 0, 0, tiled=True
    ).reshape(LINE * token_count, WIDE)
    line, given = lax.optimization_barrier((line, given))

    sent, mix = dispatch(line, kept, given)
    taken = lax.all_to_all(
        sent.reshape(2 * PLANE, KEEP, D + SIDE), CROSS_AXES, 0, 0, tiled=True
    ).reshape(2 * PLANE * KEEP, D + SIDE)

    served = expert(taken, gate_w[0], up_w[0], down_w[0])

    served, taken = lax.optimization_barrier((served, taken))
    beside = turned(taken)
    served, beside = lax.optimization_barrier((served, beside))
    back = lax.all_to_all(
        served.reshape(2 * PLANE, KEEP, D), CROSS_AXES, 0, 0, tiled=True
    ).reshape(2 * PLANE * KEEP, D)

    mixed = combine(mix, back, beside)
    gathered = lax.all_to_all(
        mixed.reshape(LINE, token_count, -1), LINE_AXES, 0, 0, tiled=True
    ).reshape(mixed.shape)
    context, moe_out = finish(
        assign,
        lengths,
        gathered,
        queries[0].reshape(slot_dev, STEPS * heads, -1),
        new_kv[0],
    )
    return (
        context.reshape(1, slot_dev, STEPS, heads, LAT),
        moe_out.reshape(1, slot_dev, STEPS, D),
    )


def solution(mesh):
    fine = Mesh(
        mesh.devices.reshape(2, Y, XH, LINE, ZL, CORE), ("pool", "y", "xh", "zh", "zl", "core")
    )
    return jax.shard_map(
        on_device,
        mesh=fine,
        in_specs=(
            P("pool", None, EP_AXES, None),
            P("pool", None, EP_AXES, None),
            P(),
            P(),
            P("pool", EP_AXES, None, None, None),
            P("pool", EP_AXES, None, None),
            P("pool", EP_AXES, None, None),
            P("pool", EP_AXES, None, None),
            P("pool", EP_AXES, None, None),
            P(EP_AXES, None, "pool"),
            P(EP_AXES, None, "pool"),
            P(EP_AXES, "pool", None),
        ),
        out_specs=(P("pool", EP_AXES, None, None, None), P("pool", EP_AXES, None, None)),
        check_vma=False,
    )
```

time: 182 us -> 167 us (0.918)
  blocking collectives: 157 us -> 132 us
  starting transfers between devices: 2.04 us -> 10.2 us
  waiting for transfers between devices: 0.01 us -> 6.79 us
  local copies, waits for them, and re-layouts: 5.54 us -> 2.99 us
    all_gather x1 -> x0, blocking collectives: 23.6 us -> none  [on_device(): line = lax.all_gather(token_rows, LINE_AXES, axis=0, tiled=True)]
    all_to_all x2 -> x1, blocking collectives: 32.9 us -> 18.4 us  [on_device(): lax.all_to_all(mixed.reshape(LINE, token_count, -1), LINE_AXES, 0, 0, til...]
    all_to_all x0 -> x1, starting transfers between devices: none -> 9.01 us  [on_device(): lax.all_to_all(token_rows.reshape(LINE, token_count, WIDE), LINE_AXES, 0,...]
    all_to_all x1, blocking collectives: 54.7 us -> 62.5 us  [on_device(): lax.all_to_all(sent.reshape(2 * PLANE, KEEP, D + SIDE), CROSS_AXES, 0, 0,...]
    all_to_all x1, blocking collectives: 46.2 us -> 51.5 us  [on_device(): lax.all_to_all(served.reshape(2 * PLANE, KEEP, D), CROSS_AXES, 0, 0, tile...]
    ppermute x1, waiting for transfers between devices: 0.01 us -> 4.45 us  [on_device(): given = lax.ppermute(given, 'pool', [(0, 1), (1, 0)])]
    unnamed x20 -> x16, local copies, waits for them, and re-layouts: 5.54 us -> 2.99 us
    all_to_all x0 -> x1, waiting for transfers between devices: none -> 2.34 us  [on_device(): lax.all_to_all(token_rows.reshape(LINE, token_count, WIDE), LINE_AXES, 0,...]
  transfers between devices with their start and end apart: 1 -> 2, of which waited for: 0 -> 2; matrix products, arithmetic and copies ran while one was open for 0% -> 0% of each run, Pallas kernels for 0% -> 0%
where the time goes in v3:
time: 167 us; the launch traced here: 166 us
  blocking collectives  132 us (79%)
  Pallas kernels  13.2 us (8%)
  starting transfers between devices  10.2 us (6%)
  waiting for transfers between devices  6.79 us (4%)
  local copies, waits for them, and re-layouts  2.99 us (2%)
    all_to_all x1, blocking collectives, on_device(): lax.all_to_all(sent.reshape(2 * PLANE, KEEP, D + SIDE), CROSS_AXES, 0, 0,...  62.5 us
    all_to_all x1, blocking collectives, on_device(): lax.all_to_all(served.reshape(2 * PLANE, KEEP, D), CROSS_AXES, 0, 0, tile...  51.5 us
    all_to_all x1, blocking collectives, on_device(): lax.all_to_all(mixed.reshape(LINE, token_count, -1), LINE_AXES, 0, 0, til...  18.4 us
    all_to_all x1, starting transfers between devices, on_device(): lax.all_to_all(token_rows.reshape(LINE, token_count, WIDE), LINE_AXES, 0,...  9.01 us
    pallas_call x1, Pallas kernels, expert(): pl.pallas_call(expert_kernel, out_shape=jax.ShapeDtypeStruct((count, D),...  6.28 us
    ppermute x1, waiting for transfers between devices, on_device(): given = lax.ppermute(given, 'pool', [(0, 1), (1, 0)])  4.45 us
  transfers between devices with their start and end apart: 2, of which 2 were waited for; matrix products, arithmetic and copies ran while one was open for 0% of the time, Pallas kernels for 0%

profile of v3, /device:TPU:1, one launch (start us, length us, event | category | flops | bytes accessed | tf_op | source)
XLA Modules:
  0.0 166.3 jit_solution(14366520026318527502)
XLA Ops:
  0.6 2.2 %prepare.1 = (bf16[256,384]{1,0:T(8,128)(2,1)}, bf16[256,384]{1,0:T(8,128)(2,1)}, bf16[32,3712]{1,0:T(8,128)(2,1)}) custom-call(s32[2,256]{1,0:T(2,128)} %assign_ref.3, bf16[576,256]{1,0:T(8,128)(2,1)} %bitcast.39, bf16[4,256]{1,0:T(4,128)(2,1)} %bitcast.44, bf16[2,4,3584]{2,1,0:T(4,128)(2,1)} %bitcast.41, s32[2,4,8]{2,1,0:T(4,128)} %bitcast.42, ...), custom_call_target="tpu_custom_call" | custom-call | tf_op jit(solution)/shard_map/prepare/pallas_call | solution.py:260
  2.8 9.0 %all-to-all-start = ((bf16[4,8,3712]{2,1,0:T(8,128)(2,1)}), bf16[4,8,3712]{2,1,0:T(8,128)(2,1)S(1)}, u32[]{:S(2)}, u32[]{:S(2)}) async-start(bf16[4,8,3712]{2,1,0:T(8,128)(2,1)} %bitcast.40), calls=%async_computation | async-start | bytes 475136 | tf_op jit(solution)/shard_map/all_to_all | solution.py:388
  11.8 1.2 collective-permute-start
  13.0 4.5 %collective-permute-done.given_ref = bf16[256,384]{1,0:T(8,128)(2,1)S(1)} collective-permute-done((bf16[256,384]{1,0:T(8,128)(2,1)}, bf16[256,384]{1,0:T(8,128)(2,1)S(1)}, u32[]{:S(2)}, u32[]{:S(2)}) %collective-permute-start) | collective-permute-done | bytes 196640 | tf_op jit(solution)/shard_map/ppermute | solution.py:387
  17.5 2.3 %all-to-all-done = bf16[4,8,3712]{2,1,0:T(8,128)(2,1)S(1)} async-done(((bf16[4,8,3712]{2,1,0:T(8,128)(2,1)}), bf16[4,8,3712]{2,1,0:T(8,128)(2,1)S(1)}, u32[]{:S(2)}, u32[]{:S(2)}) %all-to-all-start) | async-done | bytes 237600 | tf_op jit(solution)/shard_map/all_to_all | solution.py:388
  19.8 0.0 copy-start.1
  19.8 0.9 copy-done.1
  20.7 0.9 dispatch.1
  21.6 0.0 copy-start.5
  21.6 0.0 copy-start.6
  21.6 62.5 %all_to_all.20 = bf16[64,8,3968]{2,1,0:T(8,128)(2,1)S(1)} all-to-all(bf16[64,8,3968]{2,1,0:T(8,128)(2,1)S(1)} %bitcast.29), channel_id=1, replica_groups=mesh['pool'=2,'y'=4,'xh'=2,'zh'=4,'zl'=2,'core'=2] {'pool','y','xh','zl'..., dimensions={0} | all-to-all | bytes 8126464 | tf_op jit(solution)/shard_map/all_to_all | solution.py:394
  84.1 0.0 copy-done.5
  84.1 0.0 copy-done.6
  84.1 2.0 %copy-done.7 = bf16[1,512,3584]{2,1,0:T(8,128)(2,1)S(1)} copy-done((bf16[1,512,3584]{2,1,0:T(8,128)(2,1)S(1)}, bf16[1,512,3584]{2,1,0:T(8,128)(2,1)}, u32[]{:S(2)}) %copy-start.7) | copy-done | bytes 3670040
  86.2 6.3 %expert.1 = bf16[512,3584]{1,0:T(8,128)(2,1)S(1)} custom-call(bf16[512,3968]{1,0:T(8,128)(2,1)S(1)} %bitcast.24, bf16[3584,512]{1,0:T(8,128)(2,1)S(1)} %bitcast.36, bf16[3584,512]{1,0:T(8,128)(2,1)S(1)} %bitcast.37, bf16[512,3584]{1,0:T(8,128)(2,1)S(1)} %bitcast.38), custom_call_target="tpu_custom_call" | custom-call | flops 5637144576 | bytes 18350080 | tf_op jit(solution)/shard_map/expert/pallas_call | solution.py:164
  92.5 0.2 turned.1.beside_ref
  92.7 51.5 %all_to_all.21 = bf16[64,8,3584]{2,1,0:T(8,128)(2,1)S(1)} all-to-all(bf16[64,8,3584]{2,1,0:T(8,128)(2,1)S(1)} %bitcast.30), channel_id=1, replica_groups=mesh['pool'=2,'y'=4,'xh'=2,'zh'=4,'zl'=2,'core'=2] {'pool','y','xh','zl'..., dimensions={0} | all-to-all | bytes 7340032 | tf_op jit(solution)/shard_map/all_to_all | solution.py:403
  144.3 1.4 combine.1
  145.6 18.4 %all_to_all.22 = bf16[4,8,8704]{2,1,0:T(8,128)(2,1)S(1)} all-to-all(bf16[4,8,8704]{2,1,0:T(8,128)(2,1)S(1)} %bitcast.31), channel_id=1, replica_groups=mesh['pool'=2,'y'=4,'xh'=2,'zh'=4,'zl'=2,'core'=2] {'zh'}, dimensions={0} | all-to-all | bytes 1114112 | tf_op jit(solution)/shard_map/all_to_all | solution.py:408
  164.0 0.0 copy-done
  164.0 0.0 copy-done.2
  164.0 0.0 copy-done.3
  164.0 0.0 copy-done.4
  164.0 2.3 %finish.1 = (bf16[2,256,512]{2,1,0:T(8,128)(2,1)}, bf16[2,4,3584]{2,1,0:T(4,128)(2,1)}) custom-call(s32[2,256]{1,0:T(2,128)S(1)} %copy-done.3, s32[2,256]{1,0:T(2,128)S(1)} %copy-done.4, bf16[32,8704]{1,0:T(8,128)(2,1)S(1)} %bitcast.32, bf16[2,256,576]{2,1,0:T(8,128)(2,1)S(1)} %bitcast.34, bf16[2,4,576]{2,1,0:T(4,128)(2,1)S(1)} %bitcast.35), custom_call_target="tpu_custom_call" | custom-call | tf_op jit(solution)/shard_map/finish/pallas_call | solution.py:350
  (5 shorter events, 0.0 us)
Async XLA Ops:
  2.8 17.0 %all-to-all-start = ((bf16[4,8,3712]{2,1,0:T(8,128)(2,1)}), bf16[4,8,3712]{2,1,0:T(8,128)(2,1)S(1)}, u32[]{:S(2)}, u32[]{:S(2)}) async-start(bf16[4,8,3712]{2,1,0:T(8,128)(2,1)} %bitcast.40), calls=%async_computation | async-start | bytes 475136 | tf_op jit(solution)/shard_map/all_to_all | solution.py:388
  11.8 5.7 %collective-permute-start = (bf16[256,384]{1,0:T(8,128)(2,1)}, bf16[256,384]{1,0:T(8,128)(2,1)S(1)}, u32[]{:S(2)}, u32[]{:S(2)}) collective-permute-start(bf16[256,384]{1,0:T(8,128)(2,1)} %get-tuple-element.16), channel_id=1, source_target_pairs={{0,128},{128,0},{1,129},{129,1},{2,130},{130,2},{3,131},{131,3},{4... | collective-permute-start | bytes 589832 | tf_op jit(solution)/shard_map/ppermute | solution.py:387
  19.8 0.9 copy-start.1
  21.6 62.5 %copy-start.5 = (bf16[1,3584,512]{2,1,0:T(8,128)(2,1)S(1)}, bf16[1,3584,512]{2,1,0:T(8,128)(2,1)}, u32[]{:S(2)}) copy-start(bf16[1,3584,512]{2,1,0:T(8,128)(2,1)} %param.21) | copy-start | bytes 11010052
  21.6 62.5 %copy-start.6 = (bf16[1,3584,512]{2,1,0:T(8,128)(2,1)S(1)}, bf16[1,3584,512]{2,1,0:T(8,128)(2,1)}, u32[]{:S(2)}) copy-start(bf16[1,3584,512]{2,1,0:T(8,128)(2,1)} %param.22) | copy-start | bytes 11010052
  84.1 2.0 %copy-start.7 = (bf16[1,512,3584]{2,1,0:T(8,128)(2,1)S(1)}, bf16[1,512,3584]{2,1,0:T(8,128)(2,1)}, u32[]{:S(2)}) copy-start(bf16[1,512,3584]{2,1,0:T(8,128)(2,1)} %param.23) | copy-start | bytes 11010052
  144.3 19.7 %copy-start = (bf16[1,2,4,64,576]{4,3,2,1,0:T(8,128)(2,1)S(1)}, bf16[1,2,4,64,576]{4,3,2,1,0:T(8,128)(2,1)}, u32[]{:S(2)}) copy-start(bf16[1,2,4,64,576]{4,3,2,1,0:T(8,128)(2,1)} %param.16) | copy-start | bytes 1769476
  144.3 19.7 %copy-start.2 = (bf16[1,2,4,576]{3,2,1,0:T(4,128)(2,1)S(1)}, bf16[1,2,4,576]{3,2,1,0:T(4,128)(2,1)}, u32[]{:S(2)}) copy-start(bf16[1,2,4,576]{3,2,1,0:T(4,128)(2,1)} %param.17) | copy-start | bytes 27652
  144.3 19.7 %copy-start.3 = (s32[2,256]{1,0:T(2,128)S(1)}, s32[2,256]{1,0:T(2,128)}, u32[]{:S(2)}) copy-start(s32[2,256]{1,0:T(2,128)} %assign_ref.3) | copy-start | bytes 6148
  144.3 19.7 %copy-start.4 = (s32[2,256]{1,0:T(2,128)S(1)}, s32[2,256]{1,0:T(2,128)}, u32[]{:S(2)}) copy-start(s32[2,256]{1,0:T(2,128)} %lengths_ref.1) | copy-start | bytes 6148

commit v4 on v3

--- a/solution.py
+++ b/solution.py
@@ -38,8 +38,15 @@
     return pl.BlockSpec(shape, lambda i: (0,) * len(shape))
 
 
-def dispatch_kernel(line_ref, kept_ref, given_ref, sent_ref, mix_ref):
+def dispatch_kernel(line_ref, kept_ref, given_ref, sent_ref, mix_ref, done):
     group, zh = lax.axis_index("pool"), lax.axis_index(LINE_AXES)
+    count = PLANE * KEEP
+    copies = []
+    for index, (half, ref) in enumerate(((group, given_ref), (1 - group, kept_ref))):
+        top = pl.multiple_of(half * count, count)
+        target = sent_ref.at[pl.ds(top, count), pl.ds(D, SIDE)]
+        copies.append(pltpu.make_async_copy(ref, target, done.at[index]))
+        copies[index].start()
     tokens = line_ref.shape[0]
     routing = jnp.concatenate(
         [line_ref[:, pl.ds(D, 128)].astype(jnp.float32), jnp.zeros((128 - tokens, 128), jnp.float32)],
@@ -77,16 +84,14 @@
             same, part, (((1,), (1,)), ((), ())), preferred_element_type=jnp.float32
         ).astype(jnp.bfloat16)
         mix_ref[index] = jnp.concatenate([across, across], axis=1)
-    count = PLANE * KEEP
     for start in range(0, D, BLOCK):
         columns = pl.ds(start, BLOCK)
         rows = jnp.dot(choose, line_ref[:, columns], preferred_element_type=jnp.float32)
         rows = rows.astype(jnp.bfloat16)
         sent_ref[pl.ds(0, count), columns] = rows
         sent_ref[pl.ds(count, count), columns] = rows
-    for half, ref in ((group, given_ref), (1 - group, kept_ref)):
-        top = pl.multiple_of(half * count, count)
-        sent_ref[pl.ds(top, count), pl.ds(D, SIDE)] = ref[...]
+    for copy in copies:
+        copy.wait()
 
 
 def dispatch(line, kept, given):
@@ -99,8 +104,9 @@
             jax.ShapeDtypeStruct((count, D + SIDE), jnp.bfloat16),
             jax.ShapeDtypeStruct((2, tokens, count), jnp.bfloat16),
         ),
-        in_specs=[vmem, vmem, vmem],
+        in_specs=[vmem, pl.BlockSpec(memory_space=pltpu.HBM), pl.BlockSpec(memory_space=pl.ANY)],
         out_specs=(vmem, vmem),
+        scratch_shapes=[pltpu.SemaphoreType.DMA((2,))],
         compiler_params=pltpu.CompilerParams(vmem_limit_bytes=24 * MIB),
         cost_estimate=pl.CostEstimate(
             flops=2 * count * tokens * D, bytes_accessed=8 * count * D, transcendentals=0
@@ -140,52 +146,61 @@
     )(taken, taken, taken)
 
 
-def expert_kernel(taken_ref, gate_ref, up_ref, down_ref, out_ref, inner, down, done):
-    copy = pltpu.make_async_copy(down_ref, down, done)
-    copy.start()
-    width = inner.shape[1]
-    for start in range(0, width, 256):
+def inner_kernel(taken_ref, gate_ref, up_ref, inner_ref):
+    for start in range(0, inner_ref.shape[1], 256):
         columns = pl.ds(start, 256)
         rows = taken_ref[:, pl.ds(0, D)]
         gate = jnp.dot(rows, gate_ref[:, columns], preferred_element_type=jnp.float32)
         up = jnp.dot(rows, up_ref[:, columns], preferred_element_type=jnp.float32)
-        inner[:, columns] = (jax.nn.silu(gate) * up).astype(jnp.bfloat16)
-    copy.wait()
+        inner_ref[:, columns] = (jax.nn.silu(gate) * up).astype(jnp.bfloat16)
+
+
+def served_kernel(inner_ref, down_ref, out_ref):
     for start in range(0, D, BLOCK):
         columns = pl.ds(start, BLOCK)
         out_ref[:, columns] = jnp.dot(
-            inner[...], down[:, columns], preferred_element_type=jnp.float32
+            inner_ref[...], down_ref[:, columns], preferred_element_type=jnp.float32
         ).astype(jnp.bfloat16)
 
 
 def expert(taken, gate, up, down):
     count, width = taken.shape[0], gate.shape[1]
     vmem = pl.BlockSpec(memory_space=pltpu.VMEM)
-    return pl.pallas_call(
-        expert_kernel,
+    inner = pl.pallas_call(
+        inner_kernel,
+        out_shape=jax.ShapeDtypeStruct((count, width), jnp.bfloat16),
+        in_specs=[vmem, vmem, vmem],
+        out_specs=vmem,
+        compiler_params=pltpu.CompilerParams(vmem_limit_bytes=20 * MIB),
+        cost_estimate=pl.CostEstimate(
+            flops=4 * count * width * D,
+            bytes_accessed=4 * width * D + 2 * count * (D + width),
+            transcendentals=count * width,
+        ),
+        name="inner",
+    )(taken, gate, up)
+    return pl.pallas_call(
+        served_kernel,
         out_shape=jax.ShapeDtypeStruct((count, D), jnp.bfloat16),
-        in_specs=[vmem, vmem, vmem, pl.BlockSpec(memory_space=pl.ANY)],
+        in_specs=[vmem, vmem],
         out_specs=vmem,
-        scratch_shapes=[
-            pltpu.VMEM((count, width), jnp.bfloat16),
-            pltpu.VMEM((width, D), jnp.bfloat16),
-            pltpu.SemaphoreType.DMA,
-        ],
-        compiler_params=pltpu.CompilerParams(vmem_limit_bytes=28 * MIB),
+        compiler_params=pltpu.CompilerParams(vmem_limit_bytes=16 * MIB),
         cost_estimate=pl.CostEstimate(
-            flops=6 * count * width * D, bytes_accessed=6 * width * D + 4 * count * D, transcendentals=0
-        ),
-        name="expert",
-    )(taken, gate, up, down)
+            flops=2 * count * width * D,
+            bytes_accessed=2 * width * D + 2 * count * (D + width),
+            transcendentals=0,
+        ),
+        name="served",
+    )(inner, down)
 
 
 def combine_kernel(mix_ref, back_ref, beside_ref, out_ref):
+    tokens = mix_ref.shape[1]
+    mix = jnp.concatenate([mix_ref[0], mix_ref[1]], axis=0)
     for start in range(0, D, BLOCK):
         columns = pl.ds(start, BLOCK)
-        back = back_ref[:, columns]
-        total = jnp.dot(mix_ref[0], back, preferred_element_type=jnp.float32)
-        total = total + jnp.dot(mix_ref[1], back, preferred_element_type=jnp.float32)
-        out_ref[:, columns] = total.astype(jnp.bfloat16)
+        both = jnp.dot(mix, back_ref[:, columns], preferred_element_type=jnp.float32)
+        out_ref[:, columns] = (both[:tokens] + both[tokens:]).astype(jnp.bfloat16)
     out_ref[:, pl.ds(D, beside_ref.shape[1])] = beside_ref[...]
 
 

time: 167 us -> 164 us (0.982)
  local copies, waits for them, and re-layouts: 2.99 us -> 0.96 us
    unnamed x16, local copies, waits for them, and re-layouts: 2.99 us -> 0.96 us
    pallas_call x1 -> x2, Pallas kernels: 6.28 us -> 6.02 us  [the longest x1 3.95 us: expert(): pl.pallas_call(inner_kernel, out_shape=jax.ShapeDtypeStruct((count, width...]
where the time goes in v4:
time: 164 us
  blocking collectives  132 us (80%)
  Pallas kernels  12.4 us (8%)
  starting transfers between devices  10.2 us (6%)
  waiting for transfers between devices  6.79 us (4%)
    all_to_all x1, blocking collectives, on_device(): lax.all_to_all(sent.reshape(2 * PLANE, KEEP, D + SIDE), CROSS_AXES, 0, 0,...  62.5 us
    all_to_all x1, blocking collectives, on_device(): lax.all_to_all(served.reshape(2 * PLANE, KEEP, D), CROSS_AXES, 0, 0, tile...  51.5 us
    all_to_all x1, blocking collectives, on_device(): lax.all_to_all(mixed.reshape(LINE, token_count, -1), LINE_AXES, 0, 0, til...  18.4 us
    all_to_all x1, starting transfers between devices, on_device(): lax.all_to_all(token_rows.reshape(LINE, token_count, WIDE), LINE_AXES, 0,...  9.01 us
    ppermute x1, waiting for transfers between devices, on_device(): given = lax.ppermute(given, 'pool', [(0, 1), (1, 0)])  4.45 us
    pallas_call x1, Pallas kernels, expert(): pl.pallas_call(inner_kernel, out_shape=jax.ShapeDtypeStruct((count, width...  3.95 us
  transfers between devices with their start and end apart: 2, of which 2 were waited for; matrix products, arithmetic and copies ran while one was open for 0% of the time, Pallas kernels for 0%

profile of v4, /device:TPU:1, one launch (start us, length us, event | category | flops | bytes accessed | tf_op | source)
XLA Modules:
  0.0 163.5 jit_solution(5193928480161803781)
XLA Ops:
  0.6 2.2 %prepare.1 = (bf16[256,384]{1,0:T(8,128)(2,1)}, bf16[256,384]{1,0:T(8,128)(2,1)}, bf16[32,3712]{1,0:T(8,128)(2,1)}) custom-call(s32[2,256]{1,0:T(2,128)} %assign_ref.3, bf16[576,256]{1,0:T(8,128)(2,1)} %bitcast.39, bf16[4,256]{1,0:T(4,128)(2,1)} %bitcast.44, bf16[2,4,3584]{2,1,0:T(4,128)(2,1)} %bitcast.41, s32[2,4,8]{2,1,0:T(4,128)} %bitcast.42, ...), custom_call_target="tpu_custom_call" | custom-call | tf_op jit(solution)/shard_map/prepare/pallas_call | solution.py:275
  2.8 9.0 %all-to-all-start = ((bf16[4,8,3712]{2,1,0:T(8,128)(2,1)}), bf16[4,8,3712]{2,1,0:T(8,128)(2,1)S(1)}, u32[]{:S(2)}, u32[]{:S(2)}) async-start(bf16[4,8,3712]{2,1,0:T(8,128)(2,1)} %bitcast.40), calls=%async_computation | async-start | bytes 475136 | tf_op jit(solution)/shard_map/all_to_all | solution.py:403
  11.8 1.2 collective-permute-start
  13.0 4.5 %collective-permute-done.given_ref = bf16[256,384]{1,0:T(8,128)(2,1)S(1)} collective-permute-done((bf16[256,384]{1,0:T(8,128)(2,1)}, bf16[256,384]{1,0:T(8,128)(2,1)S(1)}, u32[]{:S(2)}, u32[]{:S(2)}) %collective-permute-start) | collective-permute-done | bytes 196640 | tf_op jit(solution)/shard_map/ppermute | solution.py:402
  17.5 2.3 %all-to-all-done = bf16[4,8,3712]{2,1,0:T(8,128)(2,1)S(1)} async-done(((bf16[4,8,3712]{2,1,0:T(8,128)(2,1)}), bf16[4,8,3712]{2,1,0:T(8,128)(2,1)S(1)}, u32[]{:S(2)}, u32[]{:S(2)}) %all-to-all-start) | async-done | bytes 237600 | tf_op jit(solution)/shard_map/all_to_all | solution.py:403
  19.8 0.9 copy-done.2
  20.7 0.9 dispatch.1
  21.7 0.0 copy-start.6
  21.7 0.0 copy-start.7
  21.7 62.5 %all_to_all.20 = bf16[64,8,3968]{2,1,0:T(8,128)(2,1)S(1)} all-to-all(bf16[64,8,3968]{2,1,0:T(8,128)(2,1)S(1)} %bitcast.30), channel_id=1, replica_groups=mesh['pool'=2,'y'=4,'xh'=2,'zh'=4,'zl'=2,'core'=2] {'pool','y','xh','zl'..., dimensions={0} | all-to-all | bytes 8126464 | tf_op jit(solution)/shard_map/all_to_all | solution.py:409
  84.2 0.0 copy-done.6
  84.2 0.0 copy-done.7
  84.2 4.0 %inner.1.inner_ref = bf16[512,512]{1,0:T(8,128)(2,1)S(1)} custom-call(bf16[512,3968]{1,0:T(8,128)(2,1)S(1)} %bitcast.24, bf16[3584,512]{1,0:T(8,128)(2,1)S(1)} %bitcast.37, bf16[3584,512]{1,0:T(8,128)(2,1)S(1)} %bitcast.38), custom_call_target="tpu_custom_call" | custom-call | flops 3758096384 | bytes 11534336 | tf_op jit(solution)/shard_map/inner/pallas_call | solution.py:169
  88.2 0.0 copy-done
  88.2 2.1 %served.1 = bf16[512,3584]{1,0:T(8,128)(2,1)S(1)} custom-call(bf16[512,512]{1,0:T(8,128)(2,1)S(1)} %inner.1.inner_ref, bf16[512,3584]{1,0:T(8,128)(2,1)S(1)} %bitcast.31), custom_call_target="tpu_custom_call" | custom-call | flops 1879048192 | bytes 7864320 | tf_op jit(solution)/shard_map/served/pallas_call | solution.py:182
  90.2 0.2 turned.1.beside_ref
  90.5 51.5 %all_to_all.21 = bf16[64,8,3584]{2,1,0:T(8,128)(2,1)S(1)} all-to-all(bf16[64,8,3584]{2,1,0:T(8,128)(2,1)S(1)} %bitcast.29), channel_id=1, replica_groups=mesh['pool'=2,'y'=4,'xh'=2,'zh'=4,'zl'=2,'core'=2] {'pool','y','xh','zl'..., dimensions={0} | all-to-all | bytes 7340032 | tf_op jit(solution)/shard_map/all_to_all | solution.py:418
  142.1 0.7 combine.1
  142.8 18.4 %all_to_all.22 = bf16[4,8,8704]{2,1,0:T(8,128)(2,1)S(1)} all-to-all(bf16[4,8,8704]{2,1,0:T(8,128)(2,1)S(1)} %bitcast.32), channel_id=1, replica_groups=mesh['pool'=2,'y'=4,'xh'=2,'zh'=4,'zl'=2,'core'=2] {'zh'}, dimensions={0} | all-to-all | bytes 1114112 | tf_op jit(solution)/shard_map/all_to_all | solution.py:423
  161.2 0.0 copy-done.1
  161.2 0.0 copy-done.3
  161.2 0.0 copy-done.4
  161.2 0.0 copy-done.5
  161.2 2.3 %finish.1 = (bf16[2,256,512]{2,1,0:T(8,128)(2,1)}, bf16[2,4,3584]{2,1,0:T(4,128)(2,1)}) custom-call(s32[2,256]{1,0:T(2,128)S(1)} %copy-done.4, s32[2,256]{1,0:T(2,128)S(1)} %copy-done.5, bf16[32,8704]{1,0:T(8,128)(2,1)S(1)} %bitcast.33, bf16[2,256,576]{2,1,0:T(8,128)(2,1)S(1)} %bitcast.35, bf16[2,4,576]{2,1,0:T(4,128)(2,1)S(1)} %bitcast.36), custom_call_target="tpu_custom_call" | custom-call | tf_op jit(solution)/shard_map/finish/pallas_call | solution.py:365
  (6 shorter events, 0.0 us)
Async XLA Ops:
  2.8 17.0 %all-to-all-start = ((bf16[4,8,3712]{2,1,0:T(8,128)(2,1)}), bf16[4,8,3712]{2,1,0:T(8,128)(2,1)S(1)}, u32[]{:S(2)}, u32[]{:S(2)}) async-start(bf16[4,8,3712]{2,1,0:T(8,128)(2,1)} %bitcast.40), calls=%async_computation | async-start | bytes 475136 | tf_op jit(solution)/shard_map/all_to_all | solution.py:403
  11.8 5.7 %collective-permute-start = (bf16[256,384]{1,0:T(8,128)(2,1)}, bf16[256,384]{1,0:T(8,128)(2,1)S(1)}, u32[]{:S(2)}, u32[]{:S(2)}) collective-permute-start(bf16[256,384]{1,0:T(8,128)(2,1)} %get-tuple-element.16), channel_id=1, source_target_pairs={{0,128},{128,0},{1,129},{129,1},{2,130},{130,2},{3,131},{131,3},{4... | collective-permute-start | bytes 589832 | tf_op jit(solution)/shard_map/ppermute | solution.py:402
  19.8 0.9 copy-start.2
  21.7 62.5 %copy-start.6 = (bf16[1,3584,512]{2,1,0:T(8,128)(2,1)S(1)}, bf16[1,3584,512]{2,1,0:T(8,128)(2,1)}, u32[]{:S(2)}) copy-start(bf16[1,3584,512]{2,1,0:T(8,128)(2,1)} %param.21) | copy-start | bytes 11010052
  21.7 62.5 %copy-start.7 = (bf16[1,3584,512]{2,1,0:T(8,128)(2,1)S(1)}, bf16[1,3584,512]{2,1,0:T(8,128)(2,1)}, u32[]{:S(2)}) copy-start(bf16[1,3584,512]{2,1,0:T(8,128)(2,1)} %param.22) | copy-start | bytes 11010052
  84.2 4.0 %copy-start = (bf16[1,512,3584]{2,1,0:T(8,128)(2,1)S(1)}, bf16[1,512,3584]{2,1,0:T(8,128)(2,1)}, u32[]{:S(2)}) copy-start(bf16[1,512,3584]{2,1,0:T(8,128)(2,1)} %param.23) | copy-start | bytes 11010052
  142.0 19.1 %copy-start.1 = (bf16[1,2,4,64,576]{4,3,2,1,0:T(8,128)(2,1)S(1)}, bf16[1,2,4,64,576]{4,3,2,1,0:T(8,128)(2,1)}, u32[]{:S(2)}) copy-start(bf16[1,2,4,64,576]{4,3,2,1,0:T(8,128)(2,1)} %param.16) | copy-start | bytes 1769476
  142.0 19.1 %copy-start.3 = (bf16[1,2,4,576]{3,2,1,0:T(4,128)(2,1)S(1)}, bf16[1,2,4,576]{3,2,1,0:T(4,128)(2,1)}, u32[]{:S(2)}) copy-start(bf16[1,2,4,576]{3,2,1,0:T(4,128)(2,1)} %param.17) | copy-start | bytes 27652
  142.0 19.1 %copy-start.4 = (s32[2,256]{1,0:T(2,128)S(1)}, s32[2,256]{1,0:T(2,128)}, u32[]{:S(2)}) copy-start(s32[2,256]{1,0:T(2,128)} %assign_ref.3) | copy-start | bytes 6148
  142.1 19.1 %copy-start.5 = (s32[2,256]{1,0:T(2,128)S(1)}, s32[2,256]{1,0:T(2,128)}, u32[]{:S(2)}) copy-start(s32[2,256]{1,0:T(2,128)} %lengths_ref.1) | copy-start | bytes 6148

commit v5 on v4

--- a/solution.py
+++ b/solution.py
@@ -405,6 +405,7 @@
     ).reshape(LINE * token_count, WIDE)
     line, given = lax.optimization_barrier((line, given))
 
+    kept = pltpu.with_memory_space_constraint(kept, pltpu.HBM)
     sent, mix = dispatch(line, kept, given)
     taken = lax.all_to_all(
         sent.reshape(2 * PLANE, KEEP, D + SIDE), CROSS_AXES, 0, 0, tiled=True

time: 164 us -> 163 us (level)
  no operation moved by 1% of the time
where the time goes in v5:
time: 163 us
  blocking collectives  132 us (81%)
  Pallas kernels  12.5 us (8%)
  starting transfers between devices  10.2 us (6%)
  waiting for transfers between devices  6.79 us (4%)
    all_to_all x1, blocking collectives, on_device(): lax.all_to_all(sent.reshape(2 * PLANE, KEEP, D + SIDE), CROSS_AXES, 0, 0,...  62.5 us
    all_to_all x1, blocking collectives, on_device(): lax.all_to_all(served.reshape(2 * PLANE, KEEP, D), CROSS_AXES, 0, 0, tile...  51.5 us
    all_to_all x1, blocking collectives, on_device(): lax.all_to_all(mixed.reshape(LINE, token_count, -1), LINE_AXES, 0, 0, til...  18.3 us
    all_to_all x1, starting transfers between devices, on_device(): lax.all_to_all(token_rows.reshape(LINE, token_count, WIDE), LINE_AXES, 0,...  9.01 us
    ppermute x1, waiting for transfers between devices, on_device(): given = lax.ppermute(given, 'pool', [(0, 1), (1, 0)])  4.45 us
    pallas_call x1, Pallas kernels, expert(): pl.pallas_call(inner_kernel, out_shape=jax.ShapeDtypeStruct((count, width...  3.95 us
  transfers between devices with their start and end apart: 2, of which 2 were waited for; matrix products, arithmetic and copies ran while one was open for 0% of the time, Pallas kernels for 0%

profile of v5, /device:TPU:1, one launch (start us, length us, event | category | flops | bytes accessed | tf_op | source)
XLA Modules:
  0.0 162.6 jit_solution(585655675072454890)
XLA Ops:
  0.6 2.2 %prepare.1 = (bf16[256,384]{1,0:T(8,128)(2,1)}, bf16[256,384]{1,0:T(8,128)(2,1)}, bf16[32,3712]{1,0:T(8,128)(2,1)}) custom-call(s32[2,256]{1,0:T(2,128)} %assign_ref.3, bf16[576,256]{1,0:T(8,128)(2,1)} %bitcast.39, bf16[4,256]{1,0:T(4,128)(2,1)} %bitcast.44, bf16[2,4,3584]{2,1,0:T(4,128)(2,1)} %bitcast.41, s32[2,4,8]{2,1,0:T(4,128)} %bitcast.42, ...), custom_call_target="tpu_custom_call" | custom-call | tf_op jit(solution)/shard_map/prepare/pallas_call | solution.py:275
  2.8 9.0 %all-to-all-start = ((bf16[4,8,3712]{2,1,0:T(8,128)(2,1)}), bf16[4,8,3712]{2,1,0:T(8,128)(2,1)S(1)}, u32[]{:S(2)}, u32[]{:S(2)}) async-start(bf16[4,8,3712]{2,1,0:T(8,128)(2,1)} %bitcast.40), calls=%async_computation | async-start | bytes 475136 | tf_op jit(solution)/shard_map/all_to_all | solution.py:403
  11.8 1.2 collective-permute-start
  13.0 4.5 %collective-permute-done.given_ref = bf16[256,384]{1,0:T(8,128)(2,1)S(1)} collective-permute-done((bf16[256,384]{1,0:T(8,128)(2,1)}, bf16[256,384]{1,0:T(8,128)(2,1)S(1)}, u32[]{:S(2)}, u32[]{:S(2)}) %collective-permute-start) | collective-permute-done | bytes 196640 | tf_op jit(solution)/shard_map/ppermute | solution.py:402
  17.5 2.3 %all-to-all-done = bf16[4,8,3712]{2,1,0:T(8,128)(2,1)S(1)} async-done(((bf16[4,8,3712]{2,1,0:T(8,128)(2,1)}), bf16[4,8,3712]{2,1,0:T(8,128)(2,1)S(1)}, u32[]{:S(2)}, u32[]{:S(2)}) %all-to-all-start) | async-done | bytes 237600 | tf_op jit(solution)/shard_map/all_to_all | solution.py:403
  19.8 1.0 dispatch.1
  20.8 0.0 copy-start.5
  20.8 0.0 copy-start.6
  20.8 62.5 %all_to_all.20 = bf16[64,8,3968]{2,1,0:T(8,128)(2,1)S(1)} all-to-all(bf16[64,8,3968]{2,1,0:T(8,128)(2,1)S(1)} %bitcast.30), channel_id=1, replica_groups=mesh['pool'=2,'y'=4,'xh'=2,'zh'=4,'zl'=2,'core'=2] {'pool','y','xh','zl'..., dimensions={0} | all-to-all | bytes 8126464 | tf_op jit(solution)/shard_map/all_to_all | solution.py:410
  83.3 0.0 copy-done.5
  83.3 0.0 copy-done.6
  83.3 4.0 %inner.1.inner_ref = bf16[512,512]{1,0:T(8,128)(2,1)S(1)} custom-call(bf16[512,3968]{1,0:T(8,128)(2,1)S(1)} %bitcast.24, bf16[3584,512]{1,0:T(8,128)(2,1)S(1)} %bitcast.37, bf16[3584,512]{1,0:T(8,128)(2,1)S(1)} %bitcast.38), custom_call_target="tpu_custom_call" | custom-call | flops 3758096384 | bytes 11534336 | tf_op jit(solution)/shard_map/inner/pallas_call | solution.py:169
  87.3 0.0 copy-done
  87.3 2.1 %served.1 = bf16[512,3584]{1,0:T(8,128)(2,1)S(1)} custom-call(bf16[512,512]{1,0:T(8,128)(2,1)S(1)} %inner.1.inner_ref, bf16[512,3584]{1,0:T(8,128)(2,1)S(1)} %bitcast.31), custom_call_target="tpu_custom_call" | custom-call | flops 1879048192 | bytes 7864320 | tf_op jit(solution)/shard_map/served/pallas_call | solution.py:182
  89.4 0.2 turned.1.beside_ref
  89.6 51.5 %all_to_all.21 = bf16[64,8,3584]{2,1,0:T(8,128)(2,1)S(1)} all-to-all(bf16[64,8,3584]{2,1,0:T(8,128)(2,1)S(1)} %bitcast.29), channel_id=1, replica_groups=mesh['pool'=2,'y'=4,'xh'=2,'zh'=4,'zl'=2,'core'=2] {'pool','y','xh','zl'..., dimensions={0} | all-to-all | bytes 7340032 | tf_op jit(solution)/shard_map/all_to_all | solution.py:419
  141.2 0.0 copy-start.1
  141.2 0.7 combine.1
  141.9 18.3 %all_to_all.22 = bf16[4,8,8704]{2,1,0:T(8,128)(2,1)S(1)} all-to-all(bf16[4,8,8704]{2,1,0:T(8,128)(2,1)S(1)} %bitcast.32), channel_id=1, replica_groups=mesh['pool'=2,'y'=4,'xh'=2,'zh'=4,'zl'=2,'core'=2] {'zh'}, dimensions={0} | all-to-all | bytes 1114112 | tf_op jit(solution)/shard_map/all_to_all | solution.py:424
  160.3 0.0 copy-done.1
  160.3 0.0 copy-done.2
  160.3 0.0 copy-done.3
  160.3 0.0 copy-done.4
  160.3 2.3 %finish.1 = (bf16[2,256,512]{2,1,0:T(8,128)(2,1)}, bf16[2,4,3584]{2,1,0:T(4,128)(2,1)}) custom-call(s32[2,256]{1,0:T(2,128)S(1)} %copy-done.3, s32[2,256]{1,0:T(2,128)S(1)} %copy-done.4, bf16[32,8704]{1,0:T(8,128)(2,1)S(1)} %bitcast.33, bf16[2,256,576]{2,1,0:T(8,128)(2,1)S(1)} %bitcast.35, bf16[2,4,576]{2,1,0:T(4,128)(2,1)S(1)} %bitcast.36), custom_call_target="tpu_custom_call" | custom-call | tf_op jit(solution)/shard_map/finish/pallas_call | solution.py:365
  (4 shorter events, 0.0 us)
Async XLA Ops:
  2.8 17.0 %all-to-all-start = ((bf16[4,8,3712]{2,1,0:T(8,128)(2,1)}), bf16[4,8,3712]{2,1,0:T(8,128)(2,1)S(1)}, u32[]{:S(2)}, u32[]{:S(2)}) async-start(bf16[4,8,3712]{2,1,0:T(8,128)(2,1)} %bitcast.40), calls=%async_computation | async-start | bytes 475136 | tf_op jit(solution)/shard_map/all_to_all | solution.py:403
  11.8 5.7 %collective-permute-start = (bf16[256,384]{1,0:T(8,128)(2,1)}, bf16[256,384]{1,0:T(8,128)(2,1)S(1)}, u32[]{:S(2)}, u32[]{:S(2)}) collective-permute-start(bf16[256,384]{1,0:T(8,128)(2,1)} %get-tuple-element.16), channel_id=1, source_target_pairs={{0,128},{128,0},{1,129},{129,1},{2,130},{130,2},{3,131},{131,3},{4... | collective-permute-start | bytes 589832 | tf_op jit(solution)/shard_map/ppermute | solution.py:402
  20.8 62.5 %copy-start.5 = (bf16[1,3584,512]{2,1,0:T(8,128)(2,1)S(1)}, bf16[1,3584,512]{2,1,0:T(8,128)(2,1)}, u32[]{:S(2)}) copy-start(bf16[1,3584,512]{2,1,0:T(8,128)(2,1)} %param.21) | copy-start | bytes 11010052
  20.8 62.5 %copy-start.6 = (bf16[1,3584,512]{2,1,0:T(8,128)(2,1)S(1)}, bf16[1,3584,512]{2,1,0:T(8,128)(2,1)}, u32[]{:S(2)}) copy-start(bf16[1,3584,512]{2,1,0:T(8,128)(2,1)} %param.22) | copy-start | bytes 11010052
  83.3 4.0 %copy-start = (bf16[1,512,3584]{2,1,0:T(8,128)(2,1)S(1)}, bf16[1,512,3584]{2,1,0:T(8,128)(2,1)}, u32[]{:S(2)}) copy-start(bf16[1,512,3584]{2,1,0:T(8,128)(2,1)} %param.23) | copy-start | bytes 11010052
  141.2 19.1 %copy-start.1 = (bf16[1,2,4,64,576]{4,3,2,1,0:T(8,128)(2,1)S(1)}, bf16[1,2,4,64,576]{4,3,2,1,0:T(8,128)(2,1)}, u32[]{:S(2)}) copy-start(bf16[1,2,4,64,576]{4,3,2,1,0:T(8,128)(2,1)} %param.16) | copy-start | bytes 1769476
  141.2 19.1 %copy-start.2 = (bf16[1,2,4,576]{3,2,1,0:T(4,128)(2,1)S(1)}, bf16[1,2,4,576]{3,2,1,0:T(4,128)(2,1)}, u32[]{:S(2)}) copy-start(bf16[1,2,4,576]{3,2,1,0:T(4,128)(2,1)} %param.17) | copy-start | bytes 27652
  141.2 19.1 %copy-start.3 = (s32[2,256]{1,0:T(2,128)S(1)}, s32[2,256]{1,0:T(2,128)}, u32[]{:S(2)}) copy-start(s32[2,256]{1,0:T(2,128)} %assign_ref.3) | copy-start | bytes 6148
  141.2 19.1 %copy-start.4 = (s32[2,256]{1,0:T(2,128)S(1)}, s32[2,256]{1,0:T(2,128)}, u32[]{:S(2)}) copy-start(s32[2,256]{1,0:T(2,128)} %lengths_ref.1) | copy-start | bytes 6148

commit v6 on v5

--- a/solution.py
+++ b/solution.py
@@ -115,24 +115,39 @@
     )(line, kept, given)
 
 
+def rows_of(count):
+    return count // (SPREAD * KEEP)
+
+
 def turn_kernel(one_ref, two_ref, three_ref, out_ref):
     rows = out_ref.shape[0]
     group = SPREAD * KEEP
     to = lax.broadcasted_iota(jnp.int32, (rows, group), 0)
     at = lax.broadcasted_iota(jnp.int32, (rows, group), 1)
     first = to % SPREAD * KEEP + to // SPREAD
-    for index in range(out_ref.shape[1] // ROW):
+    blocks = rows_of(one_ref.shape[0])
+    out_ref[:, pl.ds(blocks * (LAT + ROPE), 128)] = jnp.zeros((rows, 128), jnp.bfloat16)
+    for index in range(blocks):
         block = pl.ds(index * group, group)
         three = jnp.concatenate([r[block, :] for r in (one_ref, two_ref, three_ref)], axis=1)
-        for part, (start, width) in enumerate(((0, SIDE), (SIDE, ROW - SIDE))):
+        for part, width in enumerate((SIDE, ROW - SIDE)):
             turn = jnp.where(at == first + part * LINE, 1.0, 0.0).astype(jnp.bfloat16)
             moved = jnp.dot(turn, three[:, :width], preferred_element_type=jnp.float32)
-            out_ref[:, pl.ds(index * ROW + start, width)] = moved.astype(jnp.bfloat16)
+            moved = moved.astype(jnp.bfloat16)
+            if part == 0:
+                out_ref[:, pl.ds(index * LAT, SIDE)] = moved
+            else:
+                rest, scales = LAT - SIDE, LAT // QB
+                out_ref[:, pl.ds(index * LAT + SIDE, rest)] = moved[:, :rest]
+                out_ref[:, pl.ds(blocks * LAT + index * ROPE, ROPE)] = moved[:, rest : rest + ROPE]
+                out_ref[:, pl.ds(blocks * (LAT + ROPE) + index * scales, scales)] = moved[
+                    :, rest + ROPE : rest + ROPE + scales
+                ]
 
 
 def turned(taken):
     rows = taken.shape[0]
-    shape = (LINE * SPREAD, rows // (SPREAD * KEEP) * ROW)
+    shape = (LINE * SPREAD, rows_of(rows) * (LAT + ROPE) + 128)
     return pl.pallas_call(
         turn_kernel,
         grid=(1,),
@@ -307,20 +322,23 @@
     step = lax.broadcasted_iota(jnp.int32, (rows, new), 0) // (rows // STEPS)
     token = lax.broadcasted_iota(jnp.int32, (rows, new), 1)
     by_rows = (((1,), (1,)), ((), ()))
+    scales = gathered_ref[:, pl.ds(D + slot_dev * parts * (LAT + ROPE), 128)]
+    scales = scales.astype(jnp.float32).T
     for b in range(slot_dev):
         slot = ep_index * slot_dev + b
         length = jnp.sum(jnp.where(assigned == slot, lengths, 0), axis=1, keepdims=True)
+        held = [b * parts + part for part in range(parts)]
+        every = slot_dev * parts
         keys = jnp.concatenate(
-            [
-                gathered_ref[:, pl.ds(D + (b * parts + part) * ROW, ROW)]
-                for part in range(parts)
-            ],
-            axis=0,
-        )
-        scale = keys[:, LAT:].astype(jnp.float32).T[ROPE : ROPE + blocks]
+            [gathered_ref[:, pl.ds(D + at * LAT, LAT)] for at in held], axis=0
+        )
+        ropes = jnp.concatenate(
+            [gathered_ref[:, pl.ds(D + every * LAT + at * ROPE, ROPE)] for at in held], axis=0
+        )
+        scale = jnp.concatenate([scales[at * blocks : (at + 1) * blocks] for at in held], axis=1)
         score = lax.dot_general(
             query_ref[b, :, pl.ds(LAT, ROPE)],
-            keys[:, LAT : LAT + ROPE],
+            ropes,
             by_rows,
             preferred_element_type=jnp.float32,
         )

time: 163 us -> 163 us (level)
  no operation moved by 1% of the time
where the time goes in v6:
time: 163 us; the launch traced here: 162 us
  blocking collectives  132 us (81%)
  Pallas kernels  12.5 us (8%)
  starting transfers between devices  10.2 us (6%)
  waiting for transfers between devices  6.79 us (4%)
    all_to_all x1, blocking collectives, on_device(): lax.all_to_all(sent.reshape(2 * PLANE, KEEP, D + SIDE), CROSS_AXES, 0, 0,...  62.5 us
    all_to_all x1, blocking collectives, on_device(): lax.all_to_all(served.reshape(2 * PLANE, KEEP, D), CROSS_AXES, 0, 0, tile...  51.5 us
    all_to_all x1, blocking collectives, on_device(): lax.all_to_all(mixed.reshape(LINE, token_count, -1), LINE_AXES, 0, 0, til...  18 us
    all_to_all x1, starting transfers between devices, on_device(): lax.all_to_all(token_rows.reshape(LINE, token_count, WIDE), LINE_AXES, 0,...  9.01 us
    ppermute x1, waiting for transfers between devices, on_device(): given = lax.ppermute(given, 'pool', [(0, 1), (1, 0)])  4.45 us
    pallas_call x1, Pallas kernels, expert(): pl.pallas_call(inner_kernel, out_shape=jax.ShapeDtypeStruct((count, width...  3.95 us
  transfers between devices with their start and end apart: 2, of which 2 were waited for; matrix products, arithmetic and copies ran while one was open for 0% of the time, Pallas kernels for 0%

profile of v6, /device:TPU:1, one launch (start us, length us, event | category | flops | bytes accessed | tf_op | source)
XLA Modules:
  0.0 162.3 jit_solution(11062112958824081449)
XLA Ops:
  0.6 2.2 %prepare.1 = (bf16[256,384]{1,0:T(8,128)(2,1)}, bf16[256,384]{1,0:T(8,128)(2,1)}, bf16[32,3712]{1,0:T(8,128)(2,1)}) custom-call(s32[2,256]{1,0:T(2,128)} %assign_ref.3, bf16[576,256]{1,0:T(8,128)(2,1)} %bitcast.39, bf16[4,256]{1,0:T(4,128)(2,1)} %bitcast.44, bf16[2,4,3584]{2,1,0:T(4,128)(2,1)} %bitcast.41, s32[2,4,8]{2,1,0:T(4,128)} %bitcast.42, ...), custom_call_target="tpu_custom_call" | custom-call | tf_op jit(solution)/shard_map/prepare/pallas_call | solution.py:290
  2.8 9.0 %all-to-all-start = ((bf16[4,8,3712]{2,1,0:T(8,128)(2,1)}), bf16[4,8,3712]{2,1,0:T(8,128)(2,1)S(1)}, u32[]{:S(2)}, u32[]{:S(2)}) async-start(bf16[4,8,3712]{2,1,0:T(8,128)(2,1)} %bitcast.40), calls=%async_computation | async-start | bytes 475136 | tf_op jit(solution)/shard_map/all_to_all | solution.py:421
  11.8 1.2 collective-permute-start
  13.0 4.5 %collective-permute-done.given_ref = bf16[256,384]{1,0:T(8,128)(2,1)S(1)} collective-permute-done((bf16[256,384]{1,0:T(8,128)(2,1)}, bf16[256,384]{1,0:T(8,128)(2,1)S(1)}, u32[]{:S(2)}, u32[]{:S(2)}) %collective-permute-start) | collective-permute-done | bytes 196640 | tf_op jit(solution)/shard_map/ppermute | solution.py:420
  17.5 2.3 %all-to-all-done = bf16[4,8,3712]{2,1,0:T(8,128)(2,1)S(1)} async-done(((bf16[4,8,3712]{2,1,0:T(8,128)(2,1)}), bf16[4,8,3712]{2,1,0:T(8,128)(2,1)S(1)}, u32[]{:S(2)}, u32[]{:S(2)}) %all-to-all-start) | async-done | bytes 237600 | tf_op jit(solution)/shard_map/all_to_all | solution.py:421
  19.8 1.0 dispatch.1
  20.8 0.0 copy-start.5
  20.8 0.0 copy-start.6
  20.8 62.5 %all_to_all.20 = bf16[64,8,3968]{2,1,0:T(8,128)(2,1)S(1)} all-to-all(bf16[64,8,3968]{2,1,0:T(8,128)(2,1)S(1)} %bitcast.30), channel_id=1, replica_groups=mesh['pool'=2,'y'=4,'xh'=2,'zh'=4,'zl'=2,'core'=2] {'pool','y','xh','zl'..., dimensions={0} | all-to-all | bytes 8126464 | tf_op jit(solution)/shard_map/all_to_all | solution.py:428
  83.3 0.0 copy-done.5
  83.3 0.0 copy-done.6
  83.3 0.0 copy-start
  83.3 4.0 %inner.1.inner_ref = bf16[512,512]{1,0:T(8,128)(2,1)S(1)} custom-call(bf16[512,3968]{1,0:T(8,128)(2,1)S(1)} %bitcast.24, bf16[3584,512]{1,0:T(8,128)(2,1)S(1)} %bitcast.37, bf16[3584,512]{1,0:T(8,128)(2,1)S(1)} %bitcast.38), custom_call_target="tpu_custom_call" | custom-call | flops 3758096384 | bytes 11534336 | tf_op jit(solution)/shard_map/inner/pallas_call | solution.py:184
  87.3 0.0 copy-done
  87.3 2.1 %served.1 = bf16[512,3584]{1,0:T(8,128)(2,1)S(1)} custom-call(bf16[512,512]{1,0:T(8,128)(2,1)S(1)} %inner.1.inner_ref, bf16[512,3584]{1,0:T(8,128)(2,1)S(1)} %bitcast.31), custom_call_target="tpu_custom_call" | custom-call | flops 1879048192 | bytes 7864320 | tf_op jit(solution)/shard_map/served/pallas_call | solution.py:197
  89.4 0.3 turned.1.beside_ref
  89.7 51.5 %all_to_all.21 = bf16[64,8,3584]{2,1,0:T(8,128)(2,1)S(1)} all-to-all(bf16[64,8,3584]{2,1,0:T(8,128)(2,1)S(1)} %bitcast.29), channel_id=1, replica_groups=mesh['pool'=2,'y'=4,'xh'=2,'zh'=4,'zl'=2,'core'=2] {'pool','y','xh','zl'..., dimensions={0} | all-to-all | bytes 7340032 | tf_op jit(solution)/shard_map/all_to_all | solution.py:437
  141.2 0.7 combine.1
  142.0 18.0 %all_to_all.22 = bf16[4,8,8320]{2,1,0:T(8,128)(2,1)S(1)} all-to-all(bf16[4,8,8320]{2,1,0:T(8,128)(2,1)S(1)} %bitcast.32), channel_id=1, replica_groups=mesh['pool'=2,'y'=4,'xh'=2,'zh'=4,'zl'=2,'core'=2] {'zh'}, dimensions={0} | all-to-all | bytes 1064960 | tf_op jit(solution)/shard_map/all_to_all | solution.py:442
  160.0 0.0 copy-done.1
  160.0 0.0 copy-done.2
  160.0 0.0 copy-done.3
  160.0 0.0 copy-done.4
  160.0 2.3 %finish.1 = (bf16[2,256,512]{2,1,0:T(8,128)(2,1)}, bf16[2,4,3584]{2,1,0:T(4,128)(2,1)}) custom-call(s32[2,256]{1,0:T(2,128)S(1)} %copy-done.3, s32[2,256]{1,0:T(2,128)S(1)} %copy-done.4, bf16[32,8320]{1,0:T(8,128)(2,1)S(1)} %bitcast.33, bf16[2,256,576]{2,1,0:T(8,128)(2,1)S(1)} %bitcast.35, bf16[2,4,576]{2,1,0:T(4,128)(2,1)S(1)} %bitcast.36), custom_call_target="tpu_custom_call" | custom-call | tf_op jit(solution)/shard_map/finish/pallas_call | solution.py:383
  (4 shorter events, 0.0 us)
Async XLA Ops:
  2.8 17.0 %all-to-all-start = ((bf16[4,8,3712]{2,1,0:T(8,128)(2,1)}), bf16[4,8,3712]{2,1,0:T(8,128)(2,1)S(1)}, u32[]{:S(2)}, u32[]{:S(2)}) async-start(bf16[4,8,3712]{2,1,0:T(8,128)(2,1)} %bitcast.40), calls=%async_computation | async-start | bytes 475136 | tf_op jit(solution)/shard_map/all_to_all | solution.py:421
  11.8 5.7 %collective-permute-start = (bf16[256,384]{1,0:T(8,128)(2,1)}, bf16[256,384]{1,0:T(8,128)(2,1)S(1)}, u32[]{:S(2)}, u32[]{:S(2)}) collective-permute-start(bf16[256,384]{1,0:T(8,128)(2,1)} %get-tuple-element.16), channel_id=1, source_target_pairs={{0,128},{128,0},{1,129},{129,1},{2,130},{130,2},{3,131},{131,3},{4... | collective-permute-start | bytes 589832 | tf_op jit(solution)/shard_map/ppermute | solution.py:420
  20.8 62.5 %copy-start.5 = (bf16[1,3584,512]{2,1,0:T(8,128)(2,1)S(1)}, bf16[1,3584,512]{2,1,0:T(8,128)(2,1)}, u32[]{:S(2)}) copy-start(bf16[1,3584,512]{2,1,0:T(8,128)(2,1)} %param.21) | copy-start | bytes 11010052
  20.8 62.5 %copy-start.6 = (bf16[1,3584,512]{2,1,0:T(8,128)(2,1)S(1)}, bf16[1,3584,512]{2,1,0:T(8,128)(2,1)}, u32[]{:S(2)}) copy-start(bf16[1,3584,512]{2,1,0:T(8,128)(2,1)} %param.22) | copy-start | bytes 11010052
  83.3 4.0 %copy-start = (bf16[1,512,3584]{2,1,0:T(8,128)(2,1)S(1)}, bf16[1,512,3584]{2,1,0:T(8,128)(2,1)}, u32[]{:S(2)}) copy-start(bf16[1,512,3584]{2,1,0:T(8,128)(2,1)} %param.23) | copy-start | bytes 11010052
  141.2 18.7 %copy-start.1 = (bf16[1,2,4,64,576]{4,3,2,1,0:T(8,128)(2,1)S(1)}, bf16[1,2,4,64,576]{4,3,2,1,0:T(8,128)(2,1)}, u32[]{:S(2)}) copy-start(bf16[1,2,4,64,576]{4,3,2,1,0:T(8,128)(2,1)} %param.16) | copy-start | bytes 1769476
  141.2 18.7 %copy-start.2 = (bf16[1,2,4,576]{3,2,1,0:T(4,128)(2,1)S(1)}, bf16[1,2,4,576]{3,2,1,0:T(4,128)(2,1)}, u32[]{:S(2)}) copy-start(bf16[1,2,4,576]{3,2,1,0:T(4,128)(2,1)} %param.17) | copy-start | bytes 27652
  141.2 18.7 %copy-start.3 = (s32[2,256]{1,0:T(2,128)S(1)}, s32[2,256]{1,0:T(2,128)}, u32[]{:S(2)}) copy-start(s32[2,256]{1,0:T(2,128)} %assign_ref.3) | copy-start | bytes 6148
  141.2 18.7 %copy-start.4 = (s32[2,256]{1,0:T(2,128)S(1)}, s32[2,256]{1,0:T(2,128)}, u32[]{:S(2)}) copy-start(s32[2,256]{1,0:T(2,128)} %lengths_ref.1) | copy-start | bytes 6148
